TPU v7x, 32 devices: a whole 2x2x4 slice. The times are simulated.
32 devices in a mesh: depth: 8 (over z, y), xr: 4 (over x, core).
Axes of the slice: x: 2, y: 2, z: 4, core: 2. Of those that a mesh axis runs over, the one named last changes fastest.
Arguments:
- sound_field: float32 [2, 512, 3584], P(None, 'depth', 'xr'), may hold values from -6 to 6
- index_start: float32 [512, 3584], P('depth', 'xr'), may hold values from 0.8 to 0.98
- index_end: float32 [512, 3584], P('depth', 'xr'), may hold values from 0.8 to 0.98
Outputs:
- stepped: float32 [2, 512, 3584], P(None, ('depth', 'xr'))
All inputs are finite; a program needn't handle non-finite values.
Results may differ from a plain program's by a relative error of at most 0.00035.
Values sent between devices are 32-bit elements; how exact they have to be, the bound alone decides.
A program may use at most 128 MiB of HBM per device.

v0:
```python
import jax
import jax.numpy as jnp
from jax import lax
from jax.sharding import PartitionSpec as P

depth_stiffness = 1.6
cross_stiffness = 1.2
numer_re = 2.857
numer_im = 0.004
denom_re = 2.857
denom_im = -0.004


def complex_multiply(left_re, left_im, right_re, right_im):
    return (left_re * right_re - left_im * right_im, left_re * right_im + left_im * right_re)


def complex_divide(left_re, left_im, right_re, right_im):
    modulus = right_re * right_re + right_im * right_im
    return (
        (left_re * right_re + left_im * right_im) / modulus,
        (left_im * right_re - left_re * right_im) / modulus,
    )


def explicit_half(padded, potential, stiffness, dim_index):
    extent = padded.shape[dim_index] - 2
    lower_cells = lax.slice_in_dim(padded, 0, extent, axis=dim_index)
    center_cells = lax.slice_in_dim(padded, 1, extent + 1, axis=dim_index)
    upper_cells = lax.slice_in_dim(padded, 2, extent + 2, axis=dim_index)
    applied = (
        stiffness * (lower_cells - 2.0 * center_cells + upper_cells)
        + potential[None] * center_cells
    )
    product_real, product_imaginary = complex_multiply(numer_re, numer_im, applied[0], applied[1])
    return jnp.stack([center_cells[0] + product_real, center_cells[1] + product_imaginary])


def matrix_identity(batch_shape):
    unit_matrix = jnp.eye(3, dtype=jnp.float32).reshape((3, 3) + (1,) * len(batch_shape))
    real_part = jnp.broadcast_to(unit_matrix, (3, 3) + tuple(batch_shape))
    return jnp.stack([real_part, jnp.zeros_like(real_part)])


def affine_identity(batch_shape):
    zeros_batch = jnp.zeros(batch_shape, jnp.float32)
    return jnp.stack(
        [jnp.stack([zeros_batch, zeros_batch]), jnp.stack([zeros_batch + 1.0, zeros_batch])]
    )


def normalized(matrix_pair):
    largest = jnp.max(jnp.abs(matrix_pair), axis=(0, 1, 2))
    return matrix_pair / largest


def matrix_combine(earlier, later):
    later_re = later[0][:, :, None]
    later_im = later[1][:, :, None]
    earlier_re = earlier[0][None]
    earlier_im = earlier[1][None]
    product_real = jnp.sum(later_re * earlier_re, axis=1) - jnp.sum(later_im * earlier_im, axis=1)
    product_imaginary = jnp.sum(later_re * earlier_im, axis=1) + jnp.sum(
        later_im * earlier_re, axis=1
    )
    return normalized(jnp.stack([product_real, product_imaginary]))


def affine_combine(earlier, later):
    offset_real, offset_imaginary = complex_multiply(
        later[1, 0], later[1, 1], earlier[0, 0], earlier[0, 1]
    )
    gradient_real, gradient_imaginary = complex_multiply(
        later[1, 0], later[1, 1], earlier[1, 0], earlier[1, 1]
    )
    return jnp.stack(
        [
            jnp.stack([later[0, 0] + offset_real, later[0, 1] + offset_imaginary]),
            jnp.stack([gradient_real, gradient_imaginary]),
        ]
    )


def exclusive_local(combine, values, identity_slice, dim_index, backward_sweep):
    inclusive = lax.associative_scan(combine, values, reverse=backward_sweep, axis=dim_index)
    extent = values.shape[dim_index]
    if backward_sweep:
        shifted = lax.slice_in_dim(inclusive, 1, extent, axis=dim_index)
        return jnp.concatenate([shifted, identity_slice], axis=dim_index)
    shifted = lax.slice_in_dim(inclusive, 0, extent - 1, axis=dim_index)
    return jnp.concatenate([identity_slice, shifted], axis=dim_index)


def solve_blocks(source, potential, stiffness, forward_link, backward_link):
    cell_count = potential.shape[0]
    batch_shape = potential.shape[1:]
    offdiagonal_real = denom_re * stiffness
    offdiagonal_imaginary = denom_im * stiffness
    diagonal_real = 1.0 + denom_re * (potential - 2.0 * stiffness)
    diagonal_imaginary = denom_im * (potential - 2.0 * stiffness)
    carried = matrix_identity(batch_shape)
    for row_position in range(cell_count):
        rows_re = carried[0]
        rows_im = carried[1]
        upper_row = complex_multiply(
            offdiagonal_real, offdiagonal_imaginary, rows_re[2], rows_im[2]
        )
        middle_left = complex_multiply(
            -offdiagonal_real, -offdiagonal_imaginary, rows_re[1], rows_im[1]
        )
        middle_right = complex_multiply(
            source[0, row_position][None], source[1, row_position][None], rows_re[2], rows_im[2]
        )
        lower_left = complex_multiply(
            -offdiagonal_real, -offdiagonal_imaginary, rows_re[0], rows_im[0]
        )
        lower_right = complex_multiply(
            diagonal_real[row_position][None],
            diagonal_imaginary[row_position][None],
            rows_re[2],
            rows_im[2],
        )
        new_re = jnp.stack(
            [upper_row[0], middle_left[0] + middle_right[0], lower_left[0] + lower_right[0]]
        )
        new_im = jnp.stack(
            [upper_row[1], middle_left[1] + middle_right[1], lower_left[1] + lower_right[1]]
        )
        carried = jnp.stack([new_re, new_im])
        if row_position % 4 == 3 or row_position == cell_count - 1:
            carried = normalized(carried)
    incoming = forward_link(carried)
    eliminator_real, eliminator_imaginary = complex_divide(
        incoming[0, 0, 2], incoming[1, 0, 2], incoming[0, 2, 2], incoming[1, 2, 2]
    )
    filler_real, filler_imaginary = complex_divide(
        incoming[0, 1, 2], incoming[1, 1, 2], incoming[0, 2, 2], incoming[1, 2, 2]
    )
    eliminator_sequence = []
    fill_list = []
    for row_position in range(cell_count):
        subdiagonal_real, subdiagonal_imaginary = complex_multiply(
            offdiagonal_real, offdiagonal_imaginary, eliminator_real, eliminator_imaginary
        )
        pivot_value_real = diagonal_real[row_position] - subdiagonal_real
        pivot_value_imaginary = diagonal_imaginary[row_position] - subdiagonal_imaginary
        eliminator_real, eliminator_imaginary = complex_divide(
            offdiagonal_real, offdiagonal_imaginary, pivot_value_real, pivot_value_imaginary
        )
        carried_re, carried_im = complex_multiply(
            offdiagonal_real, offdiagonal_imaginary, filler_real, filler_imaginary
        )
        filler_real, filler_imaginary = complex_divide(
            source[0, row_position] - carried_re,
            source[1, row_position] - carried_im,
            pivot_value_real,
            pivot_value_imaginary,
        )
        eliminator_sequence.append((eliminator_real, eliminator_imaginary))
        fill_list.append((filler_real, filler_imaginary))
    zeros_batch = jnp.zeros(batch_shape, jnp.float32)
    offset_real, offset_imaginary, gradient_real, gradient_imaginary = (
        zeros_batch,
        zeros_batch,
        zeros_batch + 1.0,
        zeros_batch,
    )
    for row_position in reversed(range(cell_count)):
        cell_eliminator = eliminator_sequence[row_position]
        cell_fill = fill_list[row_position]
        product_real, product_imaginary = complex_multiply(
            cell_eliminator[0], cell_eliminator[1], offset_real, offset_imaginary
        )
        linked_real, linked_imaginary = complex_multiply(
            cell_eliminator[0], cell_eliminator[1], gradient_real, gradient_imaginary
        )
        offset_real, offset_imaginary, gradient_real, gradient_imaginary = (
            cell_fill[0] - product_real,
            cell_fill[1] - product_imaginary,
            -linked_real,
            -linked_imaginary,
        )
    block_map = jnp.stack(
        [jnp.stack([offset_real, offset_imaginary]), jnp.stack([gradient_real, gradient_imaginary])]
    )
    after_block = backward_link(block_map)
    following_real = after_block[0, 0]
    following_imaginary = after_block[0, 1]
    unknown_real = [None] * cell_count
    unknown_imaginary = [None] * cell_count
    for row_position in reversed(range(cell_count)):
        cell_eliminator = eliminator_sequence[row_position]
        cell_fill = fill_list[row_position]
        product_real, product_imaginary = complex_multiply(
            cell_eliminator[0], cell_eliminator[1], following_real, following_imaginary
        )
        following_real = cell_fill[0] - product_real
        following_imaginary = cell_fill[1] - product_imaginary
        unknown_real[row_position] = following_real
        unknown_imaginary[row_position] = following_imaginary
    return jnp.stack([jnp.stack(unknown_real), jnp.stack(unknown_imaginary)])


def local(sound_field, index_start, index_end):
    depth_potential = (index_start - 1.0) * 0.5
    cross_potential = (index_end - 1.0) * 0.5
    gathered = (
        lax.all_to_all(sound_field, "depth", split_axis=2, concat_axis=1, tiled=True),
        lax.all_to_all(depth_potential[None], "depth", split_axis=2, concat_axis=1, tiled=True),
    )
    column_field = gathered[0]
    column_potential = gathered[1][0]
    column_cells, lane_count = column_potential.shape
    cell_count = sound_field.shape[1]
    group_count = column_cells // cell_count
    padded = jnp.pad(column_field, ((0, 0), (1, 1), (0, 0)))
    source = explicit_half(padded, column_potential, depth_stiffness, 1)
    source_blocks = source.reshape(2, group_count, cell_count, lane_count).transpose(0, 2, 1, 3)
    potential_blocks = column_potential.reshape(group_count, cell_count, lane_count).transpose(
        1, 0, 2
    )

    def forward_local(carried):
        return exclusive_local(matrix_combine, carried, matrix_identity((1, lane_count)), 3, False)

    def backward_local(block_map):
        return exclusive_local(affine_combine, block_map, affine_identity((1, lane_count)), 2, True)

    solved = solve_blocks(
        source_blocks, potential_blocks, depth_stiffness, forward_local, backward_local
    )
    solved = solved.transpose(0, 2, 1, 3).reshape(2, column_cells, lane_count)
    middle = lax.all_to_all(solved, "depth", split_axis=1, concat_axis=2, tiled=True)
    exchanged = (
        lax.all_to_all(middle, "xr", split_axis=1, concat_axis=2, tiled=True),
        lax.all_to_all(cross_potential[None], "xr", split_axis=1, concat_axis=2, tiled=True),
    )
    line_field = exchanged[0]
    line_potential = exchanged[1][0]
    line_rows, line_width = line_potential.shape
    segment = 16
    piece_count = line_width // segment
    padded_lines = jnp.pad(line_field, ((0, 0), (0, 0), (1, 1)))
    line_source = explicit_half(padded_lines, line_potential, cross_stiffness, 2)
    source_blocks = line_source.reshape(2, line_rows, piece_count, segment).transpose(0, 3, 1, 2)
    potential_blocks = line_potential.reshape(line_rows, piece_count, segment).transpose(2, 0, 1)

    def forward_lines(carried):
        return exclusive_local(matrix_combine, carried, matrix_identity((line_rows, 1)), 4, False)

    def backward_lines(block_map):
        return exclusive_local(affine_combine, block_map, affine_identity((line_rows, 1)), 3, True)

    solved_lines = solve_blocks(
        source_blocks, potential_blocks, cross_stiffness, forward_lines, backward_lines
    )
    return solved_lines.transpose(0, 2, 3, 1).reshape(2, line_rows, line_width)


def solution(mesh):
    in_specs = (P(None, "depth", "xr"), P("depth", "xr"), P("depth", "xr"))
    out_specs = P(None, ("depth", "xr"), None)
    return jax.shard_map(local, mesh=mesh, in_specs=in_specs, out_specs=out_specs, check_vma=False)
```

profile of v0, /device:TPU:0, one launch (start us, length us, event | category | flops | bytes accessed | tf_op | source)
XLA Modules:
  0.0 254.4 jit_solution(17467556994603861661)
XLA Ops:
  5.1 7.3 %all-to-all-start.1 = ((f32[8,1,7168]{2,1,0:T(1,128)}), f32[8,1,7168]{2,1,0:T(1,128)S(1)}, u32[]{:S(2)}, u32[]{:S(2)}) async-start(f32[8,1,7168]{2,1,0:T(1,128)} %reshape.21751), calls=%async_computation.1 | async-start | bytes 458752 | tf_op jit(solution)/shard_map/all_to_all | solution.py:209
  16.7 4.1 %all-to-all-done.1 = f32[8,1,7168]{2,1,0:T(1,128)S(1)} async-done(((f32[8,1,7168]{2,1,0:T(1,128)}), f32[8,1,7168]{2,1,0:T(1,128)S(1)}, u32[]{:S(2)}, u32[]{:S(2)}) %all-to-all-start.1) | async-done | bytes 229408 | tf_op jit(solution)/shard_map/all_to_all | solution.py:209
  20.8 3.5 %all-to-all-start = ((f32[8,1,14336]{2,1,0:T(1,128)}), f32[8,1,14336]{2,1,0:T(1,128)S(1)}, u32[]{:S(2)}, u32[]{:S(2)}) async-start(f32[8,1,14336]{2,1,0:T(1,128)} %reshape.21753), calls=%async_computation | async-start | bytes 917504 | tf_op jit(solution)/shard_map/all_to_all | solution.py:208
  29.9 7.1 %all-to-all-done = f32[8,1,14336]{2,1,0:T(1,128)S(1)} async-done(((f32[8,1,14336]{2,1,0:T(1,128)}), f32[8,1,14336]{2,1,0:T(1,128)S(1)}, u32[]{:S(2)}, u32[]{:S(2)}) %all-to-all-start) | async-done | bytes 458784 | tf_op jit(solution)/shard_map/all_to_all | solution.py:208
  37.0 3.9 %all-to-all-start.4 = ((f32[1,64,896]{2,0,1:T(1,128)}), f32[1,64,896]{2,0,1:T(1,128)S(1)}, u32[]{:S(2)}, u32[]{:S(2)}) async-start(f32[1,64,896]{2,0,1:T(1,128)} %copy.6375), calls=%async_computation.4 | async-start | bytes 458752 | tf_op jit(solution)/shard_map/all_to_all | solution.py:236
  60.8 3.6 %all-to-all-start.2 = ((f32[2,512,112]{2,0,1:T(2,128)}), f32[2,512,112]{2,0,1:T(2,128)S(1)}, u32[]{:S(2)}, u32[]{:S(2)}) async-start(f32[2,512,112]{2,0,1:T(2,128)} %copy.6368), calls=%async_computation.2 | async-start | bytes 1048576 | tf_op jit(solution)/shard_map/all_to_all | solution.py:233
  68.5 11.1 %all-to-all-done.2 = f32[2,512,112]{2,0,1:T(2,128)S(1)} async-done(((f32[2,512,112]{2,0,1:T(2,128)}), f32[2,512,112]{2,0,1:T(2,128)S(1)}, u32[]{:S(2)}, u32[]{:S(2)}) %all-to-all-start.2) | async-done | bytes 458784 | tf_op jit(solution)/shard_map/all_to_all | solution.py:233
  81.5 3.5 %all-to-all-start.3 = ((f32[2,64,896]{2,0,1:T(2,128)}), f32[2,64,896]{2,0,1:T(2,128)S(1)}, u32[]{:S(2)}, u32[]{:S(2)}) async-start(f32[2,64,896]{2,0,1:T(2,128)} %reshape.21678), calls=%async_computation.3 | async-start | bytes 917504 | tf_op jit(solution)/shard_map/all_to_all | solution.py:235
  85.3 7.8 %all-to-all-done.3 = f32[2,64,896]{2,0,1:T(2,128)S(1)} async-done(((f32[2,64,896]{2,0,1:T(2,128)}), f32[2,64,896]{2,0,1:T(2,128)S(1)}, u32[]{:S(2)}, u32[]{:S(2)}) %all-to-all-start.3) | async-done | bytes 458784 | tf_op jit(solution)/shard_map/all_to_all | solution.py:235
  99.7 12.5 %slice_reduce_fusion.19 = (f32[16,224]{1,0:T(8,128)S(1)}, f32[16,224]{1,0:T(8,128)S(1)}, f32[16,224]{1,0:T(8,128)S(1)}, f32[16,224]{1,0:T(8,128)S(1)}, f32[16,22...) fusion(f32[2,16,16,224]{1,3,2,0:T(8,128)S(1)} %maximum_bitcast_, ...), kind=kLoop, calls=%fused_computation.20 | loop fusion | bytes 372736 | tf_op jit(solution)/shard_map/slice | solution.py:112
  112.3 33.3 %slice_reduce_fusion.1 = (f32[16,224]{1,0:T(8,128)S(1)}, f32[16,224]{1,0:T(8,128)S(1)}, f32[16,224]{1,0:T(8,128)S(1)}, f32[16,224]{1,0:T(8,128)S(1)}, f32[16,224...) fusion(f32[2,16,16,224]{1,3,2,0:T(8,128)} %copy-done), kind=kLoop, calls=%fused_computation.2 | loop fusion | bytes 544768 | tf_op jit(solution)/shard_map/slice | solution.py:112
  148.0 4.8 %slice.3798 = f32[2,3,3,16,112]{4,3,2,1,0:T(8,128)S(1)} slice(f32[2,3,3,16,224]{4,3,2,1,0:T(8,128)S(1)} %fusion), slice={[0:2:1], [0:3:1], [0:3:1], [0:16:1], [1:224:2]} | slice | bytes 258048 | tf_op jit(solution)/shard_map/slice | solution.py:85
  152.8 4.7 %slice.3800 = f32[2,3,3,16,112]{4,3,2,1,0:T(8,128)S(1)} slice(f32[2,3,3,16,224]{4,3,2,1,0:T(8,128)S(1)} %fusion), slice={[0:2:1], [0:3:1], [0:3:1], [0:16:1], [0:223:2]} | slice | bytes 258048 | tf_op jit(solution)/shard_map/slice | solution.py:85
  157.7 2.8 %slice.3807 = f32[2,3,3,16,56]{4,3,2,1,0:T(8,128)S(1)} slice(f32[2,3,3,16,112]{4,3,2,1,0:T(8,128)S(1)} %fusion.17), slice={[0:2:1], [0:3:1], [0:3:1], [0:16:1], [1:112:2]} | slice | bytes 129024 | tf_op jit(solution)/shard_map/slice | solution.py:85
  160.5 2.6 %slice.3809 = f32[2,3,3,16,56]{4,3,2,1,0:T(8,128)S(1)} slice(f32[2,3,3,16,112]{4,3,2,1,0:T(8,128)S(1)} %fusion.17), slice={[0:2:1], [0:3:1], [0:3:1], [0:16:1], [0:111:2]} | slice | bytes 129024 | tf_op jit(solution)/shard_map/slice | solution.py:85
  192.7 2.6 %slice.3805 = f32[2,3,3,16,55]{4,3,2,1,0:T(8,128)S(1)} slice(f32[2,3,3,16,112]{4,3,2,1,0:T(8,128)S(1)} %fusion.17), slice={[0:2:1], [0:3:1], [0:3:1], [0:16:1], [2:112:2]} | slice | bytes 126720 | tf_op jit(solution)/shard_map/slice | solution.py:85
  195.3 2.3 pad.157
  200.6 3.3 %pad.158 = f32[2,3,3,16,112]{4,3,2,1,0:T(8,128)S(1)} pad(f32[2,3,3,16,56]{4,3,2,1,0:T(8,128)S(1)} %pad_maximum_fusion.22, f32[]{:T(128)} %constant.29.clone.1), padding=0_0_0x0_0_0x0_0_0x0_0_0x0_1_1 | pad | bytes 193540 | tf_op jit(solution)/shard_map/pad | solution.py:85
  203.9 3.4 %pad.159 = f32[2,3,3,16,112]{4,3,2,1,0:T(8,128)S(1)} pad(f32[2,3,3,16,56]{4,3,2,1,0:T(8,128)S(1)} %add.21933, f32[]{:T(128)} %constant.29.clone.1), padding=0_0_0x0_0_0x0_0_0x0_0_0x1_0_1 | pad | bytes 193540 | tf_op jit(solution)/shard_map/pad | solution.py:85
  207.3 4.7 %slice.3796 = f32[2,3,3,16,111]{4,3,2,1,0:T(8,128)S(1)} slice(f32[2,3,3,16,224]{4,3,2,1,0:T(8,128)S(1)} %fusion), slice={[0:2:1], [0:3:1], [0:3:1], [0:16:1], [2:224:2]} | slice | bytes 255744 | tf_op jit(solution)/shard_map/slice | solution.py:85
  212.1 5.5 %pad.1344 = f32[2,3,3,16,224]{4,3,2,1,0:T(8,128)S(1)} pad(f32[2,3,3,16,112]{4,3,2,1,0:T(8,128)S(1)} %add.21936, f32[]{:T(128)} %constant.29.clone.1), padding=0_0_0x0_0_0x0_0_0x0_0_0x1_0_1 | pad | bytes 387076
  217.9 5.5 %pad.559 = f32[2,3,3,16,223]{4,3,2,1,0:T(8,128)S(1)} pad(f32[2,3,3,16,112]{4,3,2,1,0:T(8,128)S(1)} %pad_maximum_fusion.24, f32[]{:T(128)} %constant.29.clone.1), padding=0_0_0x0_0_0x0_0_0x0_0_0x0_0_1 | pad | bytes 385924 | tf_op jit(solution)/shard_map/slice | solution.py:90
  246.7 2.4 copy.6434
  249.1 5.0 %reshape.21669 = f32[2,16,3584]{2,1,0:T(8,128)} reshape(f32[2,16,224,16]{3,2,1,0:T(8,128)} %copy.6434) | data formatting | bytes 917504 | tf_op jit(solution)/shard_map/reshape | solution.py:257
  (1146 shorter events, 100.0 us)
Async XLA Ops:
  0.0 12.4 %copy-start.3 = (f32[64,896]{1,0:T(8,128)S(1)}, f32[64,896]{1,0:T(8,128)}, u32[]{:S(2)}) copy-start(f32[64,896]{1,0:T(8,128)} %param.5) | copy-start | bytes 688132
  0.0 12.4 %copy-start.2 = (f32[2,64,896]{2,1,0:T(8,128)S(1)}, f32[2,64,896]{2,1,0:T(8,128)}, u32[]{:S(2)}) copy-start(f32[2,64,896]{2,1,0:T(8,128)} %param.3) | copy-start | bytes 1376260
  5.1 15.7 %all-to-all-start.1 = ((f32[8,1,7168]{2,1,0:T(1,128)}), f32[8,1,7168]{2,1,0:T(1,128)S(1)}, u32[]{:S(2)}, u32[]{:S(2)}) async-start(f32[8,1,7168]{2,1,0:T(1,128)} %reshape.21751), calls=%async_computation.1 | async-start | bytes 458752 | tf_op jit(solution)/shard_map/all_to_all | solution.py:209
  16.0 37.1 %copy-start.22 = (f32[3,3]{1,0:T(4,128)}, f32[3,3]{1,0:T(4,128)S(1)}, u32[]{:S(2)}) copy-start(f32[3,3]{1,0:T(4,128)S(1)} %fusion.151) | copy-start | bytes 112
  16.6 12.4 %copy-start.105 = (f32[3]{0:T(128)}, f32[3]{0:T(128)S(1)}, u32[]{:S(2)}) copy-start(f32[3]{0:T(128)S(1)} %get-tuple-element.2032) | copy-start | bytes 40
  16.6 12.4 %copy-start.107 = (f32[3]{0:T(128)}, f32[3]{0:T(128)S(1)}, u32[]{:S(2)}) copy-start(f32[3]{0:T(128)S(1)} %get-tuple-element.2033) | copy-start | bytes 40
  16.6 12.4 %copy-start.109 = (f32[3]{0:T(128)}, f32[3]{0:T(128)S(1)}, u32[]{:S(2)}) copy-start(f32[3]{0:T(128)S(1)} %get-tuple-element.2035) | copy-start | bytes 40
  16.6 12.4 %copy-start.111 = (f32[3]{0:T(128)}, f32[3]{0:T(128)S(1)}, u32[]{:S(2)}) copy-start(f32[3]{0:T(128)S(1)} %get-tuple-element.2042) | copy-start | bytes 40
  16.7 68.5 %copy-start.24 = (f32[3]{0:T(128)}, f32[3]{0:T(128)S(1)}, u32[]{:S(2)}) copy-start(f32[3]{0:T(128)S(1)} %get-tuple-element.2041) | copy-start | bytes 40
  20.8 16.2 %all-to-all-start = ((f32[8,1,14336]{2,1,0:T(1,128)}), f32[8,1,14336]{2,1,0:T(1,128)S(1)}, u32[]{:S(2)}, u32[]{:S(2)}) async-start(f32[8,1,14336]{2,1,0:T(1,128)} %reshape.21753), calls=%async_computation | async-start | bytes 917504 | tf_op jit(solution)/shard_map/all_to_all | solution.py:208
  37.0 23.9 %all-to-all-start.4 = ((f32[1,64,896]{2,0,1:T(1,128)}), f32[1,64,896]{2,0,1:T(1,128)S(1)}, u32[]{:S(2)}, u32[]{:S(2)}) async-start(f32[1,64,896]{2,0,1:T(1,128)} %copy.6375), calls=%async_computation.4 | async-start | bytes 458752 | tf_op jit(solution)/shard_map/all_to_all | solution.py:236
  60.8 18.8 %all-to-all-start.2 = ((f32[2,512,112]{2,0,1:T(2,128)}), f32[2,512,112]{2,0,1:T(2,128)S(1)}, u32[]{:S(2)}, u32[]{:S(2)}) async-start(f32[2,512,112]{2,0,1:T(2,128)} %copy.6368), calls=%async_computation.2 | async-start | bytes 1048576 | tf_op jit(solution)/shard_map/all_to_all | solution.py:233
  81.5 11.6 %all-to-all-start.3 = ((f32[2,64,896]{2,0,1:T(2,128)}), f32[2,64,896]{2,0,1:T(2,128)S(1)}, u32[]{:S(2)}, u32[]{:S(2)}) async-start(f32[2,64,896]{2,0,1:T(2,128)} %reshape.21678), calls=%async_computation.3 | async-start | bytes 917504 | tf_op jit(solution)/shard_map/all_to_all | solution.py:235
  112.2 33.4 %copy-start.25 = (f32[3]{0:T(128)S(1)}, f32[3]{0:T(128)}, u32[]{:S(2)}) copy-start(f32[3]{0:T(128)} %copy-done.24) | copy-start | bytes 40
  112.2 33.4 %copy-start.98 = (f32[3]{0:T(128)S(1)}, f32[3]{0:T(128)}, u32[]{:S(2)}) copy-start(f32[3]{0:T(128)} %get-tuple-element.2031) | copy-start | bytes 40
  112.2 33.4 %copy-start.100 = (f32[3]{0:T(128)S(1)}, f32[3]{0:T(128)}, u32[]{:S(2)}) copy-start(f32[3]{0:T(128)} %get-tuple-element.2034) | copy-start | bytes 40
  112.2 33.4 %copy-start.102 = (f32[3]{0:T(128)S(1)}, f32[3]{0:T(128)}, u32[]{:S(2)}) copy-start(f32[3]{0:T(128)} %get-tuple-element.2036) | copy-start | bytes 40
  112.2 33.4 %copy-start.104 = (f32[3]{0:T(128)S(1)}, f32[3]{0:T(128)}, u32[]{:S(2)}) copy-start(f32[3]{0:T(128)} %get-tuple-element.2037) | copy-start | bytes 40
  112.2 33.4 %copy-start.113 = (f32[3]{0:T(128)S(1)}, f32[3]{0:T(128)}, u32[]{:S(2)}) copy-start(f32[3]{0:T(128)} %get-tuple-element.2030) | copy-start | bytes 40
  112.3 33.4 %copy-start.114 = (f32[3]{0:T(128)S(1)}, f32[3]{0:T(128)}, u32[]{:S(2)}) copy-start(f32[3]{0:T(128)} %get-tuple-element.2039) | copy-start | bytes 40
  112.3 33.6 %copy-start.19 = (f32[16,224]{1,0:T(8,128)S(1)}, f32[16,224]{1,0:T(8,128)}, u32[]{:S(2)}) copy-start(f32[16,224]{1,0:T(8,128)} %get-tuple-element.1413) | copy-start | bytes 43012
  112.3 33.6 %copy-start.20 = (f32[16,224]{1,0:T(8,128)S(1)}, f32[16,224]{1,0:T(8,128)}, u32[]{:S(2)}) copy-start(f32[16,224]{1,0:T(8,128)} %get-tuple-element.1397) | copy-start | bytes 43012
  148.0 64.1 %copy-start.1 = (f32[2,3,3,16,224]{4,3,2,1,0:T(8,128)}, f32[2,3,3,16,224]{4,3,2,1,0:T(8,128)S(1)}, u32[]{:S(2)}) copy-start(f32[2,3,3,16,224]{4,3,2,1,0:T(8,128)S(1)} %fusion) | copy-start | bytes 774148
  235.1 11.0 %copy-start.21 = (f32[2,2,16,1]{3,2,1,0:T(8,128)S(1)}, f32[2,2,16,1]{3,2,1,0:T(8,128)}, u32[]{:S(2)}) copy-start(f32[2,2,16,1]{3,2,1,0:T(8,128)} %constant.82.clone.1) | copy-start | bytes 772
  (100 other events, 146.5 us)
where the time goes:
time: 259 us; the launch traced here: 254 us
  local copies, waits for them, and re-layouts  171 us (66%)
  waiting for transfers between devices  30.1 us (12%)
  other arithmetic  24.1 us (9%)
  starting transfers between devices  21.8 us (8%)
  between operations  7.23 us (3%)
    slice x9, local copies, waits for them, and re-layouts, solve_blocks(): source[0, row_position][None]  46.1 us
    slice x51, local copies, waits for them, and re-layouts, exclusive_local(): lax.associative_scan(combine, values, reverse=backward_sweep, axis=dim_in...  43.9 us
    pad x26, local copies, waits for them, and re-layouts, exclusive_local(): lax.associative_scan(combine, values, reverse=backward_sweep, axis=dim_in...  27 us
    unnamed x412, local copies, waits for them, and re-layouts  16.1 us
    all_to_all x1, waiting for transfers between devices, local(): lax.all_to_all(solved, 'depth', split_axis=1, concat_axis=2, tiled=True)  11.1 us
    all_to_all x1, waiting for transfers between devices, local(): lax.all_to_all(middle, 'xr', split_axis=1, concat_axis=2, tiled=True)  7.78 us
    all_to_all x1, starting transfers between devices, local(): lax.all_to_all(depth_potential[None], 'depth', split_axis=2, concat_axis=...  7.28 us
    all_to_all x1, waiting for transfers between devices, local(): lax.all_to_all(sound_field, 'depth', split_axis=2, concat_axis=1, tiled=T...  7.08 us
  transfers between devices with their start and end apart: 5, of which 4 were waited for; matrix products, arithmetic and copies ran while one was open for 12% of the time, Pallas kernels for 0%

commit v1 on v0

v1 whole, which is shorter than its diff:
```python
import functools

import jax
import jax.numpy as jnp
from jax import lax
from jax.experimental import pallas as pl
from jax.experimental.pallas import tpu as pltpu
from jax.sharding import PartitionSpec as P
import numpy as np

depth_stiffness = 1.6
cross_stiffness = 1.2
numer = 2.857 + 0.004j
denom = 2.857 - 0.004j
LANES = 128
SUBLANES = 8
SUMMARY_ROWS = 16
MESH = pl.DeviceIdType.MESH


class Line:
    def __init__(self, stiffness):
        shift = 1.0 / denom
        self.slope = -0.5 / stiffness
        self.level = 2.0 - shift.real / stiffness + 0.5 / stiffness
        self.damping = shift.imag / stiffness
        cosine = 0.5 * (self.level + self.slope * 0.89)
        angle = float(np.arccos(cosine))
        self.mu = complex(np.exp(0.5j * angle))
        self.nu = self.mu.conjugate()
        self.inv_det = 1.0 / (self.nu * self.nu - self.mu * self.mu)
        self.wall = -self.mu * self.mu
        self.alpha = numer / denom
        self.beta = (denom - numer) / (denom * denom * stiffness)


def mul(x, y):
    return (x[0] * y[0] - x[1] * y[1], x[0] * y[1] + x[1] * y[0])


def add(x, y):
    return (x[0] + y[0], x[1] + y[1])


def sub(x, y):
    return (x[0] - y[0], x[1] - y[1])


def cmul(c, x):
    c = complex(c)
    return (c.real * x[0] - c.imag * x[1], c.real * x[1] + c.imag * x[0])


def recip(x):
    scale = 1.0 / (x[0] * x[0] + x[1] * x[1])
    return (x[0] * scale, -x[1] * scale)


def one_minus(x):
    return (1.0 - x[0], -x[1])


def cmap(fn, x):
    return (fn(x[0]), fn(x[1]))


def step(line, coef, here, before, force=None):
    real = coef * here[0] + line.damping * here[1] - before[0]
    imag = coef * here[1] - line.damping * here[0] - before[1]
    if force is not None:
        real, imag = real + force[0], imag + force[1]
    return (real, imag)


def coefficient(line, index):
    return line.level + line.slope * index


def segment_medium(line, coefs):
    shape = coefs[0].shape
    def const(c):
        return (jnp.full(shape, c.real, jnp.float32), jnp.full(shape, c.imag, jnp.float32))
    p0, p1 = const(line.nu), const(line.mu)
    q0, q1 = const(line.mu), const(line.nu)
    for coef in coefs:
        p0, p1 = p1, step(line, coef, p1, p0)
        q0, q1 = q1, step(line, coef, q1, q0)
    lower, upper = -line.mu * line.inv_det, line.nu * line.inv_det
    t21 = add(cmul(lower, p0), cmul(upper, p1))
    t22 = add(cmul(lower, q0), cmul(upper, q1))
    t12 = add(cmul(upper, q0), cmul(lower, q1))
    t = recip(t22)
    r1 = mul(t21, t)
    r1 = (-r1[0], -r1[1])
    r2 = mul(t12, t)
    return t, r1, r2


def segment_source(line, coefs, forces, t, r2):
    zero = jnp.zeros(coefs[0].shape, jnp.float32)
    v0, v1 = (zero, zero), (zero, zero)
    for position, (coef, force) in enumerate(zip(coefs, forces)):
        if position == 0:
            v0, v1 = v1, force
        else:
            v0, v1 = v1, step(line, coef, v1, v0, force)
    lower, upper = -line.mu * line.inv_det, line.nu * line.inv_det
    right = add(cmul(upper, v0), cmul(lower, v1))
    left = add(cmul(lower, v0), cmul(upper, v1))
    s1 = mul(left, t)
    s1 = (-s1[0], -s1[1])
    s2 = sub(right, mul(r2, left))
    return s1, s2


def from_right(x, axis, amount):
    return cmap(lambda v: pltpu.roll(v, v.shape[axis] - amount, axis), x)


def from_left(x, axis, amount):
    return cmap(lambda v: pltpu.roll(v, amount, axis), x)


def medium_level(medium, axis, amount):
    t_a, r1_a, r2_a = medium
    t_b, r1_b, r2_b = (from_right(v, axis, amount) for v in medium)
    d = recip(one_minus(mul(r2_a, r1_b)))
    ra, rb = mul(d, r2_a), mul(d, r1_b)
    tad, tbd = mul(t_a, d), mul(t_b, d)
    x1, x2 = mul(t_a, rb), mul(t_b, ra)
    merged = (mul(tad, t_b), add(r1_a, mul(x1, t_a)), add(r2_b, mul(x2, t_b)))
    return merged, (d, ra, rb, t_a, t_b, tad, tbd, x1, x2)


def source_level(kept, source, axis, amount):
    d, ra, rb, t_a, t_b, tad, tbd, x1, x2 = kept
    s1_a, s2_a = source
    s1_b, s2_b = (from_right(v, axis, amount) for v in source)
    e_p = add(mul(d, s2_a), mul(ra, s1_b))
    e_q = add(mul(d, s1_b), mul(rb, s2_a))
    merged = (add(s1_a, mul(t_a, e_q)), add(s2_b, mul(t_b, e_p)))
    return merged, (e_p, e_q)


def down_level(kept, inner, p_left, q_right, axis, amount, unit):
    d, ra, rb, t_a, t_b, tad, tbd, x1, x2 = kept
    p_mid = add(add(mul(tad, p_left), mul(x2, q_right)), inner[0])
    q_mid = add(add(mul(x1, p_left), mul(tbd, q_right)), inner[1])
    shape = p_left[0].shape
    place = lax.broadcasted_iota(jnp.int32, shape, axis)
    is_left = (place % (2 * amount)) < amount
    p_moved = from_left(p_mid, axis, amount)
    q_moved = from_left(q_right, axis, amount)
    p_new = tuple(jnp.where(is_left, a, b) for a, b in zip(p_left, p_moved))
    q_new = tuple(jnp.where(is_left, a, b) for a, b in zip(q_mid, q_moved))
    return p_new, q_new


def medium_tree(medium, axis, count, unit=1):
    levels = []
    amount = unit
    while amount < count * unit:
        medium, kept = medium_level(medium, axis, amount)
        levels.append((amount, kept))
        amount *= 2
    return medium, levels


def source_tree(levels, source, axis):
    inners = []
    for amount, kept in levels:
        source, inner = source_level(kept, source, axis, amount)
        inners.append(inner)
    return source, inners


def down_tree(levels, inners, p_left, q_right, axis):
    for (amount, kept), inner in zip(reversed(levels), reversed(inners)):
        p_left, q_right = down_level(kept, inner, p_left, q_right, axis, amount, 1)
    return p_left, q_right


def between_walls(line, medium, source):
    t, r1, r2 = medium
    s1, s2 = source
    tw = cmul(line.wall, t)
    first = one_minus(cmul(line.wall, r1))
    second = one_minus(cmul(line.wall, r2))
    scale = recip(sub(mul(first, second), mul(tw, tw)))
    q_left = mul(scale, add(mul(second, s1), mul(tw, s2)))
    p_right = mul(scale, add(mul(tw, s1), mul(first, s2)))
    return cmul(line.wall, q_left), cmul(line.wall, p_right)


def segment_start(line, medium, source, p_left, q_right):
    t, r1, r2 = medium
    q_left = add(add(mul(r1, p_left), mul(t, q_right)), source[0])
    before = add(cmul(line.nu, p_left), cmul(line.mu, q_left))
    here = add(cmul(line.mu, p_left), cmul(line.nu, q_left))
    return before, here


def result(line, force, here):
    return add(cmul(line.alpha, force), cmul(line.beta, here))


def kernel(
    nd, nx, field, start, end, out,
    summary, gathered, answer, boundary, middle, received, end_received,
    tall_end, tall_field, tall_out,
    sum_send, sum_recv, ans_send, ans_recv, end_send, end_recv, mid_send, mid_recv,
):
    rows, width = start.shape[1], start.shape[0] * LANES
    tiles = width // LANES
    cells = rows // SUBLANES
    out_rows = rows // nx
    dep = lax.axis_index("depth")
    xr = lax.axis_index("xr")
    depth_line = Line(depth_stiffness)
    cross_line = Line(cross_stiffness)

    barrier = pltpu.get_barrier_semaphore()

    @pl.loop(1, nd)
    def _(offset):
        pl.semaphore_signal(barrier, 1, device_id=(lax.rem(dep + offset, nd), xr), device_id_type=MESH)

    @pl.loop(1, nx)
    def _(offset):
        pl.semaphore_signal(barrier, 1, device_id=(dep, lax.rem(xr + offset, nx)), device_id_type=MESH)

    pl.semaphore_wait(barrier, nd - 1 + nx - 1)

    def end_copy(peer, source_block):
        return pltpu.make_async_remote_copy(
            src_ref=end.at[:, pl.ds(pl.multiple_of(peer * out_rows, out_rows), out_rows), :],
            dst_ref=end_received.at[source_block],
            send_sem=end_send.at[peer],
            recv_sem=end_recv.at[source_block],
            device_id=(dep, peer),
            device_id_type=MESH,
        )

    for offset in range(1, nx):
        end_copy(lax.rem(xr + offset, nx), xr).start()

    def strided(ref, *lead):
        return [
            jnp.concatenate(
                [ref[(tile,) + lead + (pl.ds(cell, SUBLANES, stride=cells), slice(None))] for tile in range(tiles)],
                axis=1,
            )
            for cell in range(cells)
        ]

    def depth_coefs():
        return [coefficient(depth_line, v) for v in strided(start)]

    coefs = depth_coefs()
    forces = list(zip(strided(field, 0), strided(field, 1)))
    medium = segment_medium(depth_line, coefs)
    source = segment_source(depth_line, coefs, forces, medium[0], medium[2])
    total_medium, levels = medium_tree(medium, 0, SUBLANES)
    total_source, inners = source_tree(levels, source, 0)
    parts = [v for pair in (*total_medium, *total_source) for v in pair]
    for tile in range(tiles):
        for row, part in enumerate(parts):
            summary[tile, row : row + 1, :] = part[0:1, tile * LANES : (tile + 1) * LANES]

    def sum_copy(tile, origin):
        return pltpu.make_async_remote_copy(
            src_ref=summary.at[tile],
            dst_ref=gathered.at[pl.ds(pl.multiple_of(origin * SUMMARY_ROWS, SUMMARY_ROWS), SUMMARY_ROWS), :],
            send_sem=sum_send.at[tile],
            recv_sem=sum_recv.at[origin],
            device_id=(tile, xr),
            device_id_type=MESH,
        )

    for tile in range(tiles):

        @pl.when(dep != tile)
        def _():
            sum_copy(tile, dep).start()

    def tall(pieces):
        stacked = jnp.concatenate(pieces, axis=0)
        if stacked.shape[0] < LANES:
            pad = jnp.full((LANES - stacked.shape[0], LANES), 0.89, jnp.float32)
            stacked = jnp.concatenate([stacked, pad], axis=0)
        return stacked.T

    for tile in range(tiles):
        end_received[xr, tile] = end[tile, pl.ds(pl.multiple_of(xr * out_rows, out_rows), out_rows), :]
    for offset in range(nx):
        block = lax.rem(xr + offset, nx)
        if offset > 0:
            end_copy(xr, block).wait_recv()
        tall_end[pl.ds(pl.multiple_of(block * LANES, LANES), LANES), :] = tall(
            [end_received[block, tile] for tile in range(tiles)]
        )
    cross_cells = LANES // SUBLANES

    def tall_strided(ref, *lead):
        return [
            jnp.concatenate(
                [
                    ref[lead + (pl.ds(block * LANES + cell, SUBLANES, stride=cross_cells), slice(None))]
                    for block in range(nx)
                ],
                axis=1,
            )
            for cell in range(cross_cells)
        ]

    def cross_coefs():
        return [coefficient(cross_line, v) for v in tall_strided(tall_end)]

    cross_medium = segment_medium(cross_line, cross_coefs())

    def ans_copy(peer, tile):
        return pltpu.make_async_remote_copy(
            src_ref=answer.at[pl.ds(pl.multiple_of(peer * SUBLANES, SUBLANES), SUBLANES), :],
            dst_ref=boundary.at[tile],
            send_sem=ans_send.at[peer],
            recv_sem=ans_recv.at[tile],
            device_id=(peer, xr),
            device_id_type=MESH,
        )

    @pl.when(dep < tiles)
    def _():
        gathered[pl.ds(pl.multiple_of(dep * SUMMARY_ROWS, SUMMARY_ROWS), SUMMARY_ROWS), :] = summary[dep]
        for offset in range(1, nd):
            sum_copy(0, lax.rem(dep + offset, nd)).wait_recv()
        values = [gathered[pl.ds(row, nd, stride=SUMMARY_ROWS), :] for row in range(10)]
        pairs = [(values[2 * i], values[2 * i + 1]) for i in range(5)]
        all_medium, all_levels = medium_tree(tuple(pairs[:3]), 0, nd)
        all_source, all_inners = source_tree(all_levels, tuple(pairs[3:]), 0)
        p_all, q_all = between_walls(depth_line, all_medium, all_source)
        p_all, q_all = down_tree(all_levels, all_inners, p_all, q_all, 0)
        for row, value in enumerate((*p_all, *q_all)):
            answer[pl.ds(row, nd, stride=SUBLANES), :] = value
        boundary[dep] = answer[pl.ds(pl.multiple_of(dep * SUBLANES, SUBLANES), SUBLANES), :]
        for offset in range(1, nd):
            ans_copy(lax.rem(dep + offset, nd), dep).start()

    block_medium, block_levels = medium_tree(cross_medium, 0, SUBLANES)
    sub_place = lax.broadcasted_iota(jnp.int32, (SUBLANES, LANES), 0)
    lane_place = lax.broadcasted_iota(jnp.int32, (SUBLANES, LANES), 1)
    used = lane_place < tiles * out_rows

    def packed(value, fill):
        total = jnp.zeros((SUBLANES, LANES), jnp.float32)
        for block in range(nx):
            row = jnp.broadcast_to(value[0:1, block * LANES : (block + 1) * LANES], (SUBLANES, LANES))
            total = jnp.where(sub_place == block, row, total)
        return jnp.where(used, total, fill)

    def unpacked(value):
        return jnp.concatenate(
            [jnp.broadcast_to(value[block : block + 1, :], (SUBLANES, LANES)) for block in range(nx)], axis=1
        )

    slots = LANES // out_rows
    packed_medium = tuple(
        (packed(v[0], fill), packed(v[1], 0.0)) for v, fill in zip(block_medium, (1.0, 0.0, 0.0))
    )
    tile_medium, tile_levels = medium_tree(packed_medium, 1, slots, out_rows)
    line_medium, line_levels = medium_tree(tile_medium, 0, nx)

    for tile in range(tiles):

        @pl.when(dep != tile)
        def _():
            ans_copy(dep, tile).wait_recv()

    def incoming(row):
        return jnp.concatenate(
            [jnp.broadcast_to(boundary[tile, row : row + 1, :], (SUBLANES, LANES)) for tile in range(tiles)], axis=1
        )

    p_left, q_right = (incoming(0), incoming(1)), (incoming(2), incoming(3))
    p_left, q_right = down_tree(levels, inners, p_left, q_right, 0)
    all_before, all_here = segment_start(depth_line, medium, source, p_left, q_right)

    def mid_copy(tile, peer, source_block):
        return pltpu.make_async_remote_copy(
            src_ref=middle.at[tile, :, pl.ds(pl.multiple_of(peer * out_rows, out_rows), out_rows), :],
            dst_ref=received.at[source_block, tile],
            send_sem=mid_send.at[tile, peer],
            recv_sem=mid_recv.at[tile, source_block],
            device_id=(dep, peer),
            device_id_type=MESH,
        )

    for tile in range(tiles):
        cut = slice(tile * LANES, (tile + 1) * LANES)
        before = cmap(lambda v: v[:, cut], all_before)
        here = cmap(lambda v: v[:, cut], all_here)
        for cell in range(cells):
            place = pl.ds(cell, SUBLANES, stride=cells)
            force = (field[tile, 0, place, :], field[tile, 1, place, :])
            value = result(depth_line, force, here)
            middle[tile, 0, place, :] = value[0]
            middle[tile, 1, place, :] = value[1]
            if cell < cells - 1:
                coef = coefficient(depth_line, start[tile, place, :])
                before, here = here, step(depth_line, coef, here, before, force)
        for offset in range(1, nx):
            mid_copy(tile, lax.rem(xr + offset, nx), xr).start()

    own = pl.ds(pl.multiple_of(xr * out_rows, out_rows), out_rows)
    for tile in range(tiles):
        for c in range(2):
            received[xr, tile, c] = middle[tile, c, own, :]
    for offset in range(nx):
        block = lax.rem(xr + offset, nx)
        if offset > 0:
            for tile in range(tiles):
                mid_copy(tile, xr, block).wait_recv()
        for c in range(2):
            tall_field[c, pl.ds(pl.multiple_of(block * LANES, LANES), LANES), :] = tall(
                [received[block, tile, c] for tile in range(tiles)]
            )
    coefs = cross_coefs()
    forces = list(zip(tall_strided(tall_field, 0), tall_strided(tall_field, 1)))
    source = segment_source(cross_line, coefs, forces, cross_medium[0], cross_medium[2])
    block_source, block_inners = source_tree(block_levels, source, 0)
    packed_source = tuple((packed(v[0], 0.0), packed(v[1], 0.0)) for v in block_source)
    tile_source, tile_inners = source_tree(tile_levels, packed_source, 1)
    line_source, line_inners = source_tree(line_levels, tile_source, 0)
    p_left, q_right = between_walls(cross_line, line_medium, line_source)
    p_left, q_right = down_tree(line_levels, line_inners, p_left, q_right, 0)
    p_left, q_right = down_tree(tile_levels, tile_inners, p_left, q_right, 1)
    p_left, q_right = cmap(unpacked, p_left), cmap(unpacked, q_right)
    p_left, q_right = down_tree(block_levels, block_inners, p_left, q_right, 0)
    all_before, all_here = segment_start(cross_line, cross_medium, source, p_left, q_right)
    for block in range(nx):
        cut = slice(block * LANES, (block + 1) * LANES)
        before = cmap(lambda v: v[:, cut], all_before)
        here = cmap(lambda v: v[:, cut], all_here)
        for cell in range(cross_cells):
            place = pl.ds(block * LANES + cell, SUBLANES, stride=cross_cells)
            force = (tall_field[0, place, :], tall_field[1, place, :])
            value = result(cross_line, force, here)
            tall_out[0, place, :] = value[0]
            tall_out[1, place, :] = value[1]
            if cell < cross_cells - 1:
                coef = coefficient(cross_line, tall_end[place, :])
                before, here = here, step(cross_line, coef, here, before, force)
        for c in range(2):
            flat = tall_out[c, block * LANES : (block + 1) * LANES, :].T
            for tile in range(tiles):
                at = block * width + tile * LANES
                out[c, :, at : at + LANES] = flat[tile * out_rows : (tile + 1) * out_rows, :]

    for offset in range(1, nx):
        peer = lax.rem(xr + offset, nx)
        end_copy(peer, xr).wait_send()
        for tile in range(tiles):
            mid_copy(tile, peer, xr).wait_send()
    for tile in range(tiles):

        @pl.when(dep != tile)
        def _():
            sum_copy(tile, dep).wait_send()

    @pl.when(dep < tiles)
    def _():
        for offset in range(1, nd):
            ans_copy(lax.rem(dep + offset, nd), dep).wait_send()


def local(nd, nx, sound_field, index_start, index_end):
    rows, width = index_start.shape
    tiles = width // LANES
    out_rows = rows // nx
    assert tiles <= nd and tiles * out_rows <= LANES and nx <= SUBLANES
    field = sound_field.reshape(2, rows, tiles, LANES).transpose(2, 0, 1, 3)
    start = index_start.reshape(rows, tiles, LANES).transpose(1, 0, 2)
    end = index_end.reshape(rows, tiles, LANES).transpose(1, 0, 2)
    f32 = jnp.float32
    dma = pltpu.SemaphoreType.DMA
    return pl.pallas_call(
        functools.partial(kernel, nd, nx),
        out_shape=jax.ShapeDtypeStruct((2, out_rows, width * nx), f32),
        in_specs=[pl.BlockSpec(memory_space=pltpu.VMEM)] * 3,
        out_specs=pl.BlockSpec(memory_space=pltpu.VMEM),
        scratch_shapes=[
            pltpu.VMEM((tiles, SUMMARY_ROWS, LANES), f32),
            pltpu.VMEM((nd * SUMMARY_ROWS, LANES), f32),
            pltpu.VMEM((nd * SUBLANES, LANES), f32),
            pltpu.VMEM((tiles, SUBLANES, LANES), f32),
            pltpu.VMEM((tiles, 2, rows, LANES), f32),
            pltpu.VMEM((nx, tiles, 2, out_rows, LANES), f32),
            pltpu.VMEM((nx, tiles, out_rows, LANES), f32),
            pltpu.VMEM((nx * LANES, LANES), f32),
            pltpu.VMEM((2, nx * LANES, LANES), f32),
            pltpu.VMEM((2, nx * LANES, LANES), f32),
            dma((tiles,)),
            dma((nd,)),
            dma((nd,)),
            dma((tiles,)),
            dma((nx,)),
            dma((nx,)),
            dma((tiles, nx)),
            dma((tiles, nx)),
        ],
        compiler_params=pltpu.CompilerParams(
            collective_id=0, has_side_effects=True, vmem_limit_bytes=32 * 1024 * 1024
        ),
        cost_estimate=pl.CostEstimate(flops=20_000_000, bytes_accessed=2_000_000, transcendentals=0),
    )(field, start, end)


def solution(mesh):
    nd, nx = mesh.shape["depth"], mesh.shape["xr"]
    in_specs = (P(None, "depth", "xr"), P("depth", "xr"), P("depth", "xr"))
    out_specs = P(None, ("depth", "xr"), None)
    return jax.shard_map(
        functools.partial(local, nd, nx), mesh=mesh, in_specs=in_specs, out_specs=out_specs, check_vma=False
    )
```

time: 259 us -> 24.6 us (0.09); the launches traced: 254 us -> 24.5 us
  local copies, waits for them, and re-layouts: 171 us -> 1.98 us
  waiting for transfers between devices: 30.1 us -> 0 us
  other arithmetic: 24.1 us -> 0 us
  Pallas kernels: 0 us -> 22.5 us
  starting transfers between devices: 21.8 us -> 0 us
  between operations: 7.23 us -> 0.03 us
    slice x102 -> x0, local copies, waits for them, and re-layouts: 99 us -> none  [the longest x9 46.1 us: solve_blocks(): source[0, row_position][None]]
    all_to_all x5 -> x0, waiting for transfers between devices: 30.1 us -> none  [the longest x1 11.1 us: local(): lax.all_to_all(solved, 'depth', split_axis=1, concat_axis=2, tiled=True)]
    pad x26 -> x0, local copies, waits for them, and re-layouts: 27 us -> none  [exclusive_local(): lax.associative_scan(combine, values, reverse=backward_sweep, axis=dim_in...]
    pallas_call x0 -> x1, Pallas kernels: none -> 22.5 us  [local(): pl.pallas_call(functools.partial(kernel, nd, nx), out_shape=jax.ShapeDtyp...]
    all_to_all x5 -> x0, starting transfers between devices: 21.8 us -> none  [the longest x1 7.28 us: local(): lax.all_to_all(depth_potential[None], 'depth', split_axis=2, concat_axis=...]
    unnamed x412 -> x7, local copies, waits for them, and re-layouts: 16.1 us -> 1.91 us
    mul x51 -> x0, local copies, waits for them, and re-layouts: 8.17 us -> none  [the longest x5 2.61 us: complex_multiply(): left_im * right_im]
    reshape x2 -> x0, local copies, waits for them, and re-layouts: 6.24 us -> none  [the longest x1 5.04 us: local(): return solved_lines.transpose(0, 2, 3, 1).reshape(2, line_rows, line_width)]
  transfers between devices with their start and end apart: 5 -> 0, of which waited for: 4 -> 0; matrix products, arithmetic and copies ran while one was open for 12% -> 0% of each run, Pallas kernels for 0% -> 0%
where the time goes in v1:
time: 24.6 us; the launch traced here: 24.5 us
  Pallas kernels  22.5 us (91%)
  local copies, waits for them, and re-layouts  1.98 us (8%)
    pallas_call x1, Pallas kernels, local(): pl.pallas_call(functools.partial(kernel, nd, nx), out_shape=jax.ShapeDtyp...  22.5 us
    unnamed x7, local copies, waits for them, and re-layouts  1.91 us

profile of v1, /device:TPU:0, one launch (start us, length us, event | category | flops | bytes accessed | tf_op | source)
XLA Modules:
  0.0 24.5 jit_solution(11026002311378404403)
XLA Ops:
  0.0 0.0 copy-start
  0.0 0.0 copy-start.2
  0.0 0.0 copy-start.1
  0.0 1.0 %copy-done = f32[2,64,896]{2,1,0:T(8,128)S(1)} copy-done((f32[2,64,896]{2,1,0:T(8,128)S(1)}, f32[2,64,896]{2,1,0:T(8,128)}, u32[]{:S(2)}) %copy-start) | copy-done | bytes 458776
  1.1 0.0 copy-done.2
  1.1 0.1 copy-done.1
  1.2 22.5 %shard_map.37 = f32[2,16,3584]{2,1,0:T(8,128)S(1)} custom-call(f32[7,2,64,128]{3,2,1,0:T(8,128)S(1)} %bitcast_bitcast_fusion.field, f32[7,64,128]{2,1,0:T(8,128)S(1)} %get-tuple-element.6.start, f32[7,64,128]{2,1,0:T(8,128)S(1)} %get-tuple-element.5.end), custom_call_target="tpu_custom_call" | custom-call | flops 20000000 | bytes 2000000 | tf_op jit(solution)/shard_map/pallas_call | solution.py:485
  23.7 0.8 %copy.14 = f32[2,16,3584]{2,1,0:T(8,128)} copy(f32[2,16,3584]{2,1,0:T(8,128)S(1)} %shard_map.37) | data formatting | bytes 917504
  (2 shorter events, 0.1 us)
Async XLA Ops:
  0.0 1.0 %copy-start = (f32[2,64,896]{2,1,0:T(8,128)S(1)}, f32[2,64,896]{2,1,0:T(8,128)}, u32[]{:S(2)}) copy-start(f32[2,64,896]{2,1,0:T(8,128)} %param.3) | copy-start | bytes 1376260
  0.0 1.1 %copy-start.2 = (f32[64,896]{1,0:T(8,128)S(1)}, f32[64,896]{1,0:T(8,128)}, u32[]{:S(2)}) copy-start(f32[64,896]{1,0:T(8,128)} %param.5) | copy-start | bytes 688132
  0.0 1.2 %copy-start.1 = (f32[64,896]{1,0:T(8,128)S(1)}, f32[64,896]{1,0:T(8,128)}, u32[]{:S(2)}) copy-start(f32[64,896]{1,0:T(8,128)} %param.4) | copy-start | bytes 688132

commit v2 on v1

--- a/solution.py
+++ b/solution.py
@@ -121,9 +121,9 @@
     return cmap(lambda v: pltpu.roll(v, amount, axis), x)
 
 
-def medium_level(medium, axis, amount):
-    t_a, r1_a, r2_a = medium
-    t_b, r1_b, r2_b = (from_right(v, axis, amount) for v in medium)
+def merge_medium(left, right):
+    t_a, r1_a, r2_a = left
+    t_b, r1_b, r2_b = right
     d = recip(one_minus(mul(r2_a, r1_b)))
     ra, rb = mul(d, r2_a), mul(d, r1_b)
     tad, tbd = mul(t_a, d), mul(t_b, d)
@@ -132,20 +132,62 @@
     return merged, (d, ra, rb, t_a, t_b, tad, tbd, x1, x2)
 
 
-def source_level(kept, source, axis, amount):
+def merge_source(kept, left, right):
     d, ra, rb, t_a, t_b, tad, tbd, x1, x2 = kept
-    s1_a, s2_a = source
-    s1_b, s2_b = (from_right(v, axis, amount) for v in source)
+    s1_a, s2_a = left
+    s1_b, s2_b = right
     e_p = add(mul(d, s2_a), mul(ra, s1_b))
     e_q = add(mul(d, s1_b), mul(rb, s2_a))
     merged = (add(s1_a, mul(t_a, e_q)), add(s2_b, mul(t_b, e_p)))
     return merged, (e_p, e_q)
 
 
-def down_level(kept, inner, p_left, q_right, axis, amount, unit):
+def middle_waves(kept, inner, p_left, q_right):
     d, ra, rb, t_a, t_b, tad, tbd, x1, x2 = kept
     p_mid = add(add(mul(tad, p_left), mul(x2, q_right)), inner[0])
     q_mid = add(add(mul(x1, p_left), mul(tbd, q_right)), inner[1])
+    return p_mid, q_mid
+
+
+def medium_list(items):
+    levels = []
+    while len(items) > 1:
+        pairs = [merge_medium(a, b) for a, b in zip(items[0::2], items[1::2])]
+        items = [merged for merged, _ in pairs]
+        levels.append([kept for _, kept in pairs])
+    return items[0], levels
+
+
+def source_list(levels, items):
+    inners = []
+    for level in levels:
+        pairs = [merge_source(kept, a, b) for kept, a, b in zip(level, items[0::2], items[1::2])]
+        items = [merged for merged, _ in pairs]
+        inners.append([inner for _, inner in pairs])
+    return items[0], inners
+
+
+def down_list(levels, inners, p_left, q_right):
+    waves = [(p_left, q_right)]
+    for level, inner_level in zip(reversed(levels), reversed(inners)):
+        finer = []
+        for kept, inner, (p, q) in zip(level, inner_level, waves):
+            p_mid, q_mid = middle_waves(kept, inner, p, q)
+            finer += [(p, q_mid), (p_mid, q)]
+        waves = finer
+    return waves
+
+
+def medium_level(medium, axis, amount):
+    return merge_medium(medium, tuple(from_right(v, axis, amount) for v in medium))
+
+
+def source_level(kept, source, axis, amount):
+    return merge_source(kept, source, tuple(from_right(v, axis, amount) for v in source))
+
+
+def down_level(kept, inner, p_left, q_right, axis, amount):
+    p_mid, q_mid = middle_waves(kept, inner, p_left, q_right)
     shape = p_left[0].shape
     place = lax.broadcasted_iota(jnp.int32, shape, axis)
     is_left = (place % (2 * amount)) < amount
@@ -176,7 +218,7 @@
 
 def down_tree(levels, inners, p_left, q_right, axis):
     for (amount, kept), inner in zip(reversed(levels), reversed(inners)):
-        p_left, q_right = down_level(kept, inner, p_left, q_right, axis, amount, 1)
+        p_left, q_right = down_level(kept, inner, p_left, q_right, axis, amount)
     return p_left, q_right
 
 
@@ -206,14 +248,15 @@
 
 def kernel(
     nd, nx, field, start, end, out,
-    summary, gathered, answer, boundary, middle, received, end_received,
-    tall_end, tall_field, tall_out,
-    sum_send, sum_recv, ans_send, ans_recv, end_send, end_recv, mid_send, mid_recv,
+    own, received, summary, gathered, answer, boundary, edge_out, edge_in,
+    middle, tall_end, tall_field, tall_out,
+    sum_send, sum_recv, ans_send, ans_recv, bulk_send, bulk_recv, edge_send, edge_recv,
 ):
-    rows, width = start.shape[1], start.shape[0] * LANES
+    used_rows = start.shape[1]
+    width = out.shape[2] // nx
     tiles = width // LANES
-    cells = rows // SUBLANES
-    out_rows = rows // nx
+    out_rows = out.shape[1]
+    slots = LANES // out_rows
     dep = lax.axis_index("depth")
     xr = lax.axis_index("xr")
     depth_line = Line(depth_stiffness)
@@ -229,47 +272,67 @@
     def _(offset):
         pl.semaphore_signal(barrier, 1, device_id=(dep, lax.rem(xr + offset, nx)), device_id_type=MESH)
 
-    pl.semaphore_wait(barrier, nd - 1 + nx - 1)
-
-    def end_copy(peer, source_block):
+    def peer_at(offset):
+        base = xr // 2 * 2
+        return lax.rem(base + 2 * (offset // 2), nx) + lax.rem(xr + offset, 2)
+
+    RE, IM, START, END = range(4)
+
+    def at(block, part):
+        return pl.multiple_of((block * 4 + part) * LANES, LANES)
+
+    def bulk_copy(peer, source_block, part):
+        source_ref = field.at[peer, part] if part < 2 else (start if part == START else end).at[peer]
         return pltpu.make_async_remote_copy(
-            src_ref=end.at[:, pl.ds(pl.multiple_of(peer * out_rows, out_rows), out_rows), :],
-            dst_ref=end_received.at[source_block],
-            send_sem=end_send.at[peer],
-            recv_sem=end_recv.at[source_block],
+            src_ref=source_ref,
+            dst_ref=received.at[pl.ds(at(source_block, part), used_rows), :],
+            send_sem=bulk_send.at[peer, part],
+            recv_sem=bulk_recv.at[source_block, part],
             device_id=(dep, peer),
             device_id_type=MESH,
         )
 
-    for offset in range(1, nx):
-        end_copy(lax.rem(xr + offset, nx), xr).start()
-
-    def strided(ref, *lead):
-        return [
-            jnp.concatenate(
-                [ref[(tile,) + lead + (pl.ds(cell, SUBLANES, stride=cells), slice(None))] for tile in range(tiles)],
-                axis=1,
-            )
-            for cell in range(cells)
-        ]
-
-    def depth_coefs():
-        return [coefficient(depth_line, v) for v in strided(start)]
-
-    coefs = depth_coefs()
-    forces = list(zip(strided(field, 0), strided(field, 1)))
+    far_first = list(range(2, nx)) + [1]
+    pl.semaphore_wait(barrier, nd - 1 + nx - 1)
+    for part in (END, START, RE, IM):
+        for offset in far_first:
+            bulk_copy(peer_at(offset), xr, part).start()
+
+    for block in range(nx):
+        for part in range(4):
+            base = (block * 4 + part) * LANES
+            if used_rows < LANES:
+                pad = jnp.full((LANES - used_rows, LANES), 0.0 if part < 2 else 0.89, jnp.float32)
+                received[base + used_rows : base + LANES, :] = pad
+                if part < 3:
+                    own[base + used_rows : base + LANES, :] = pad
+            if part < 3:
+                own[base : base + used_rows, :] = field[block, part] if part < 2 else start[block]
+    for part in range(4):
+        received[pl.ds(at(xr, part), used_rows), :] = field[xr, part] if part < 2 else (start if part == START else end)[xr]
+
+    def wide(ref, part, row):
+        return jnp.concatenate(
+            [ref[pl.ds((block * 4 + part) * LANES + row, slots, stride=out_rows), :] for block in range(nx)], axis=1
+        )
+
+    def cut(x, block):
+        return cmap(lambda v: v[:, block * LANES : (block + 1) * LANES], x)
+
+    coefs = [coefficient(depth_line, wide(own, START, row)) for row in range(out_rows)]
+    forces = [(wide(own, RE, row), wide(own, IM, row)) for row in range(out_rows)]
     medium = segment_medium(depth_line, coefs)
     source = segment_source(depth_line, coefs, forces, medium[0], medium[2])
-    total_medium, levels = medium_tree(medium, 0, SUBLANES)
-    total_source, inners = source_tree(levels, source, 0)
-    parts = [v for pair in (*total_medium, *total_source) for v in pair]
-    for tile in range(tiles):
-        for row, part in enumerate(parts):
-            summary[tile, row : row + 1, :] = part[0:1, tile * LANES : (tile + 1) * LANES]
+    mediums = [tuple(cut(v, block) for v in medium) for block in range(nx)]
+    sources = [tuple(cut(v, block) for v in source) for block in range(nx)]
+    total_medium, levels = medium_list(mediums)
+    total_source, inners = source_list(levels, sources)
+    for row, part in enumerate(v for pair in (*total_medium, *total_source) for v in pair):
+        summary[pl.ds(row, slots, stride=SUMMARY_ROWS), :] = part
 
     def sum_copy(tile, origin):
         return pltpu.make_async_remote_copy(
-            src_ref=summary.at[tile],
+            src_ref=summary.at[pl.ds(tile * SUMMARY_ROWS, SUMMARY_ROWS), :],
             dst_ref=gathered.at[pl.ds(pl.multiple_of(origin * SUMMARY_ROWS, SUMMARY_ROWS), SUMMARY_ROWS), :],
             send_sem=sum_send.at[tile],
             recv_sem=sum_recv.at[origin],
@@ -283,22 +346,43 @@
         def _():
             sum_copy(tile, dep).start()
 
-    def tall(pieces):
-        stacked = jnp.concatenate(pieces, axis=0)
-        if stacked.shape[0] < LANES:
-            pad = jnp.full((LANES - stacked.shape[0], LANES), 0.89, jnp.float32)
-            stacked = jnp.concatenate([stacked, pad], axis=0)
-        return stacked.T
-
-    for tile in range(tiles):
-        end_received[xr, tile] = end[tile, pl.ds(pl.multiple_of(xr * out_rows, out_rows), out_rows), :]
+    def ans_copy(peer, tile):
+        return pltpu.make_async_remote_copy(
+            src_ref=answer.at[pl.ds(pl.multiple_of(peer * SUBLANES, SUBLANES), SUBLANES), :],
+            dst_ref=boundary.at[pl.ds(pl.multiple_of(tile * SUBLANES, SUBLANES), SUBLANES), :],
+            send_sem=ans_send.at[peer],
+            recv_sem=ans_recv.at[tile],
+            device_id=(peer, xr),
+            device_id_type=MESH,
+        )
+
+    if tiles < slots:
+        boundary[tiles * SUBLANES :, :] = jnp.zeros(((slots - tiles) * SUBLANES, LANES), jnp.float32)
+
+    @pl.when(dep < tiles)
+    def _():
+        gathered[pl.ds(pl.multiple_of(dep * SUMMARY_ROWS, SUMMARY_ROWS), SUMMARY_ROWS), :] = summary[
+            pl.ds(pl.multiple_of(dep * SUMMARY_ROWS, SUMMARY_ROWS), SUMMARY_ROWS), :
+        ]
+        for offset in range(1, nd):
+            sum_copy(0, lax.rem(dep + offset, nd)).wait_recv()
+        values = [gathered[pl.ds(row, nd, stride=SUMMARY_ROWS), :] for row in range(10)]
+        pairs = [(values[2 * i], values[2 * i + 1]) for i in range(5)]
+        all_medium, all_levels = medium_tree(tuple(pairs[:3]), 0, nd)
+        all_source, all_inners = source_tree(all_levels, tuple(pairs[3:]), 0)
+        p_all, q_all = between_walls(depth_line, all_medium, all_source)
+        p_all, q_all = down_tree(all_levels, all_inners, p_all, q_all, 0)
+        for row, value in enumerate((*p_all, *q_all)):
+            answer[pl.ds(row, nd, stride=SUBLANES), :] = value
+        boundary[pl.ds(pl.multiple_of(dep * SUBLANES, SUBLANES), SUBLANES), :] = answer[pl.ds(pl.multiple_of(dep * SUBLANES, SUBLANES), SUBLANES), :]
+        for offset in range(1, nd):
+            ans_copy(lax.rem(dep + offset, nd), dep).start()
+
     for offset in range(nx):
-        block = lax.rem(xr + offset, nx)
+        block = peer_at(offset)
         if offset > 0:
-            end_copy(xr, block).wait_recv()
-        tall_end[pl.ds(pl.multiple_of(block * LANES, LANES), LANES), :] = tall(
-            [end_received[block, tile] for tile in range(tiles)]
-        )
+            bulk_copy(xr, block, END).wait_recv()
+        tall_end[pl.ds(pl.multiple_of(block * LANES, LANES), LANES), :] = received[pl.ds(at(block, END), LANES), :].T
     cross_cells = LANES // SUBLANES
 
     def tall_strided(ref, *lead):
@@ -317,34 +401,6 @@
         return [coefficient(cross_line, v) for v in tall_strided(tall_end)]
 
     cross_medium = segment_medium(cross_line, cross_coefs())
-
-    def ans_copy(peer, tile):
-        return pltpu.make_async_remote_copy(
-            src_ref=answer.at[pl.ds(pl.multiple_of(peer * SUBLANES, SUBLANES), SUBLANES), :],
-            dst_ref=boundary.at[tile],
-            send_sem=ans_send.at[peer],
-            recv_sem=ans_recv.at[tile],
-            device_id=(peer, xr),
-            device_id_type=MESH,
-        )
-
-    @pl.when(dep < tiles)
-    def _():
-        gathered[pl.ds(pl.multiple_of(dep * SUMMARY_ROWS, SUMMARY_ROWS), SUMMARY_ROWS), :] = summary[dep]
-        for offset in range(1, nd):
-            sum_copy(0, lax.rem(dep + offset, nd)).wait_recv()
-        values = [gathered[pl.ds(row, nd, stride=SUMMARY_ROWS), :] for row in range(10)]
-        pairs = [(values[2 * i], values[2 * i + 1]) for i in range(5)]
-        all_medium, all_levels = medium_tree(tuple(pairs[:3]), 0, nd)
-        all_source, all_inners = source_tree(all_levels, tuple(pairs[3:]), 0)
-        p_all, q_all = between_walls(depth_line, all_medium, all_source)
-        p_all, q_all = down_tree(all_levels, all_inners, p_all, q_all, 0)
-        for row, value in enumerate((*p_all, *q_all)):
-            answer[pl.ds(row, nd, stride=SUBLANES), :] = value
-        boundary[dep] = answer[pl.ds(pl.multiple_of(dep * SUBLANES, SUBLANES), SUBLANES), :]
-        for offset in range(1, nd):
-            ans_copy(lax.rem(dep + offset, nd), dep).start()
-
     block_medium, block_levels = medium_tree(cross_medium, 0, SUBLANES)
     sub_place = lax.broadcasted_iota(jnp.int32, (SUBLANES, LANES), 0)
     lane_place = lax.broadcasted_iota(jnp.int32, (SUBLANES, LANES), 1)
@@ -362,7 +418,6 @@
             [jnp.broadcast_to(value[block : block + 1, :], (SUBLANES, LANES)) for block in range(nx)], axis=1
         )
 
-    slots = LANES // out_rows
     packed_medium = tuple(
         (packed(v[0], fill), packed(v[1], 0.0)) for v, fill in zip(block_medium, (1.0, 0.0, 0.0))
     )
@@ -375,54 +430,65 @@
         def _():
             ans_copy(dep, tile).wait_recv()
 
-    def incoming(row):
-        return jnp.concatenate(
-            [jnp.broadcast_to(boundary[tile, row : row + 1, :], (SUBLANES, LANES)) for tile in range(tiles)], axis=1
-        )
-
-    p_left, q_right = (incoming(0), incoming(1)), (incoming(2), incoming(3))
-    p_left, q_right = down_tree(levels, inners, p_left, q_right, 0)
-    all_before, all_here = segment_start(depth_line, medium, source, p_left, q_right)
-
-    def mid_copy(tile, peer, source_block):
+    edge_rows = 4 * slots
+    incoming = [boundary[pl.ds(row, slots, stride=SUBLANES), :] for row in range(4)]
+    waves = down_list(levels, inners, (incoming[0], incoming[1]), (incoming[2], incoming[3]))
+    for block, (p_left, q_right) in enumerate(waves):
+        before, here = segment_start(depth_line, mediums[block], sources[block], p_left, q_right)
+        for row, value in enumerate((*before, *here)):
+            first = block * edge_rows + row * slots
+            edge_out[first : first + slots, :] = value
+
+    def edge_at(block):
+        return pl.ds(pl.multiple_of(block * edge_rows, edge_rows), edge_rows)
+
+    def edge_copy(peer, source_block):
         return pltpu.make_async_remote_copy(
-            src_ref=middle.at[tile, :, pl.ds(pl.multiple_of(peer * out_rows, out_rows), out_rows), :],
-            dst_ref=received.at[source_block, tile],
-            send_sem=mid_send.at[tile, peer],
-            recv_sem=mid_recv.at[tile, source_block],
+            src_ref=edge_out.at[edge_at(peer), :],
+            dst_ref=edge_in.at[edge_at(source_block), :],
+            send_sem=edge_send.at[peer],
+            recv_sem=edge_recv.at[source_block],
             device_id=(dep, peer),
             device_id_type=MESH,
         )
 
-    for tile in range(tiles):
-        cut = slice(tile * LANES, (tile + 1) * LANES)
-        before = cmap(lambda v: v[:, cut], all_before)
-        here = cmap(lambda v: v[:, cut], all_here)
-        for cell in range(cells):
-            place = pl.ds(cell, SUBLANES, stride=cells)
-            force = (field[tile, 0, place, :], field[tile, 1, place, :])
+    for offset in far_first:
+        edge_copy(peer_at(offset), xr).start()
+    edge_in[edge_at(xr), :] = edge_out[edge_at(xr), :]
+
+    for group in range(0, nx, 2):
+        blocks = [peer_at(group), peer_at(group + 1)]
+        for offset, block in enumerate(blocks, group):
+            if offset > 0:
+                for part in (START, RE, IM):
+                    bulk_copy(xr, block, part).wait_recv()
+                edge_copy(xr, block).wait_recv()
+
+        def side(ref, first, **keywords):
+            return jnp.concatenate([ref[pl.ds(first(block), slots, **keywords), :] for block in blocks], axis=1)
+
+        def row_of(part, row):
+            return side(received, lambda block: at(block, part) + row, stride=out_rows)
+
+        def edge_of(row):
+            return side(edge_in, lambda block: pl.multiple_of(block * edge_rows + row * slots, SUBLANES))
+
+        before, here = (edge_of(0), edge_of(1)), (edge_of(2), edge_of(3))
+        for row in range(out_rows):
+            force = (row_of(RE, row), row_of(IM, row))
             value = result(depth_line, force, here)
-            middle[tile, 0, place, :] = value[0]
-            middle[tile, 1, place, :] = value[1]
-            if cell < cells - 1:
-                coef = coefficient(depth_line, start[tile, place, :])
+            for c in range(2):
+                for side_at in range(2):
+                    place = pl.ds((side_at * 2 + c) * LANES + row, slots, stride=out_rows)
+                    middle[place, :] = value[c][:, side_at * LANES : (side_at + 1) * LANES]
+            if row < out_rows - 1:
+                coef = coefficient(depth_line, row_of(START, row))
                 before, here = here, step(depth_line, coef, here, before, force)
-        for offset in range(1, nx):
-            mid_copy(tile, lax.rem(xr + offset, nx), xr).start()
-
-    own = pl.ds(pl.multiple_of(xr * out_rows, out_rows), out_rows)
-    for tile in range(tiles):
-        for c in range(2):
-            received[xr, tile, c] = middle[tile, c, own, :]
-    for offset in range(nx):
-        block = lax.rem(xr + offset, nx)
-        if offset > 0:
-            for tile in range(tiles):
-                mid_copy(tile, xr, block).wait_recv()
-        for c in range(2):
-            tall_field[c, pl.ds(pl.multiple_of(block * LANES, LANES), LANES), :] = tall(
-                [received[block, tile, c] for tile in range(tiles)]
-            )
+        for side_at, block in enumerate(blocks):
+            for c in range(2):
+                first = (side_at * 2 + c) * LANES
+                tall_field[c, pl.ds(pl.multiple_of(block * LANES, LANES), LANES), :] = middle[first : first + LANES, :].T
+
     coefs = cross_coefs()
     forces = list(zip(tall_strided(tall_field, 0), tall_strided(tall_field, 1)))
     source = segment_source(cross_line, coefs, forces, cross_medium[0], cross_medium[2])
@@ -437,9 +503,7 @@
     p_left, q_right = down_tree(block_levels, block_inners, p_left, q_right, 0)
     all_before, all_here = segment_start(cross_line, cross_medium, source, p_left, q_right)
     for block in range(nx):
-        cut = slice(block * LANES, (block + 1) * LANES)
-        before = cmap(lambda v: v[:, cut], all_before)
-        here = cmap(lambda v: v[:, cut], all_here)
+        before, here = cut(all_before, block), cut(all_here, block)
         for cell in range(cross_cells):
             place = pl.ds(block * LANES + cell, SUBLANES, stride=cross_cells)
             force = (tall_field[0, place, :], tall_field[1, place, :])
@@ -452,14 +516,14 @@
         for c in range(2):
             flat = tall_out[c, block * LANES : (block + 1) * LANES, :].T
             for tile in range(tiles):
-                at = block * width + tile * LANES
-                out[c, :, at : at + LANES] = flat[tile * out_rows : (tile + 1) * out_rows, :]
+                first = block * width + tile * LANES
+                out[c, :, first : first + LANES] = flat[tile * out_rows : (tile + 1) * out_rows, :]
 
     for offset in range(1, nx):
-        peer = lax.rem(xr + offset, nx)
-        end_copy(peer, xr).wait_send()
-        for tile in range(tiles):
-            mid_copy(tile, peer, xr).wait_send()
+        peer = peer_at(offset)
+        edge_copy(peer, xr).wait_send()
+        for part in range(4):
+            bulk_copy(peer, xr, part).wait_send()
     for tile in range(tiles):
 
         @pl.when(dep != tile)
@@ -476,10 +540,15 @@
     rows, width = index_start.shape
     tiles = width // LANES
     out_rows = rows // nx
-    assert tiles <= nd and tiles * out_rows <= LANES and nx <= SUBLANES
-    field = sound_field.reshape(2, rows, tiles, LANES).transpose(2, 0, 1, 3)
-    start = index_start.reshape(rows, tiles, LANES).transpose(1, 0, 2)
-    end = index_end.reshape(rows, tiles, LANES).transpose(1, 0, 2)
+    slots = LANES // out_rows
+    assert tiles <= nd and tiles <= slots and slots == SUBLANES and nx <= SUBLANES and nx % 2 == 0
+
+    def blocked(array):
+        lead = array.shape[:-2]
+        pieces = array.reshape(lead + (nx, out_rows, tiles, LANES))
+        pieces = jnp.moveaxis(jnp.swapaxes(pieces, -3, -2), len(lead), 0)
+        return pieces.reshape((nx,) + lead + (tiles * out_rows, LANES))
+
     f32 = jnp.float32
     dma = pltpu.SemaphoreType.DMA
     return pl.pallas_call(
@@ -488,13 +557,15 @@
         in_specs=[pl.BlockSpec(memory_space=pltpu.VMEM)] * 3,
         out_specs=pl.BlockSpec(memory_space=pltpu.VMEM),
         scratch_shapes=[
-            pltpu.VMEM((tiles, SUMMARY_ROWS, LANES), f32),
+            pltpu.VMEM((nx * 4 * LANES, LANES), f32),
+            pltpu.VMEM((nx * 4 * LANES, LANES), f32),
+            pltpu.VMEM((slots * SUMMARY_ROWS, LANES), f32),
             pltpu.VMEM((nd * SUMMARY_ROWS, LANES), f32),
             pltpu.VMEM((nd * SUBLANES, LANES), f32),
-            pltpu.VMEM((tiles, SUBLANES, LANES), f32),
-            pltpu.VMEM((tiles, 2, rows, LANES), f32),
-            pltpu.VMEM((nx, tiles, 2, out_rows, LANES), f32),
-            pltpu.VMEM((nx, tiles, out_rows, LANES), f32),
+            pltpu.VMEM((slots * SUBLANES, LANES), f32),
+            pltpu.VMEM((nx * 4 * slots, LANES), f32),
+            pltpu.VMEM((nx * 4 * slots, LANES), f32),
+            pltpu.VMEM((4 * LANES, LANES), f32),
             pltpu.VMEM((nx * LANES, LANES), f32),
             pltpu.VMEM((2, nx * LANES, LANES), f32),
             pltpu.VMEM((2, nx * LANES, LANES), f32),
@@ -502,16 +573,16 @@
             dma((nd,)),
             dma((nd,)),
             dma((tiles,)),
+            dma((nx, 4)),
+            dma((nx, 4)),
             dma((nx,)),
             dma((nx,)),
-            dma((tiles, nx)),
-            dma((tiles, nx)),
         ],
         compiler_params=pltpu.CompilerParams(
             collective_id=0, has_side_effects=True, vmem_limit_bytes=32 * 1024 * 1024
         ),
         cost_estimate=pl.CostEstimate(flops=20_000_000, bytes_accessed=2_000_000, transcendentals=0),
-    )(field, start, end)
+    )(blocked(sound_field), blocked(index_start), blocked(index_end))
 
 
 def solution(mesh):

time: 24.6 us -> 24.9 us (1.012)
  local copies, waits for them, and re-layouts: 1.98 us -> 3.82 us
  Pallas kernels: 22.5 us -> 20.8 us
    pallas_call x1, Pallas kernels: 22.5 us -> 20.8 us  [local(): pl.pallas_call(functools.partial(kernel, nd, nx), out_shape=jax.ShapeDtyp...]
    reshape x0 -> x3, local copies, waits for them, and re-layouts: none -> 1.16 us  [blocked(): pieces = array.reshape(lead + (nx, out_rows, tiles, LANES))]
    unnamed x7 -> x5, local copies, waits for them, and re-layouts: 1.91 us -> 2.49 us
where the time goes in v2:
time: 24.9 us; the launch traced here: 24.7 us
  Pallas kernels  20.8 us (84%)
  local copies, waits for them, and re-layouts  3.82 us (15%)
    pallas_call x1, Pallas kernels, local(): pl.pallas_call(functools.partial(kernel, nd, nx), out_shape=jax.ShapeDtyp...  20.8 us
    unnamed x5, local copies, waits for them, and re-layouts  2.49 us
    reshape x3, local copies, waits for them, and re-layouts, blocked(): pieces = array.reshape(lead + (nx, out_rows, tiles, LANES))  1.16 us

profile of v2, /device:TPU:0, one launch (start us, length us, event | category | flops | bytes accessed | tf_op | source)
XLA Modules:
  0.0 24.7 jit_solution(14353542709767568794)
XLA Ops:
  0.0 1.1 %reshape.18 = f32[2,4,16,7,128]{4,3,2,1,0:T(8,128)S(1)} reshape(f32[2,64,896]{2,1,0:T(8,128)} %param.3) | data formatting | bytes 917504 | tf_op jit(solution)/shard_map/reshape | solution.py:548
  1.1 0.0 copy-start
  1.1 0.1 copy.7
  1.2 0.8 %copy-done = f32[64,896]{1,0:T(8,128)S(1)} copy-done((f32[64,896]{1,0:T(8,128)S(1)}, f32[64,896]{1,0:T(8,128)}, u32[]{:S(2)}) %copy-start) | copy-done | bytes 229400
  2.1 0.0 copy-start.1
  2.1 0.9 %copy-done.1 = f32[64,896]{1,0:T(8,128)S(1)} copy-done((f32[64,896]{1,0:T(8,128)S(1)}, f32[64,896]{1,0:T(8,128)}, u32[]{:S(2)}) %copy-start.1) | copy-done | bytes 229400
  3.1 20.8 %shard_map.37 = f32[2,16,3584]{2,1,0:T(8,128)S(1)} custom-call(f32[4,2,112,128]{3,2,1,0:T(8,128)S(1)} %bitcast.6, f32[4,112,128]{2,1,0:T(8,128)S(1)} %bitcast.7, f32[4,112,128]{2,1,0:T(8,128)S(1)} %bitcast.8), custom_call_target="tpu_custom_call" | custom-call | flops 20000000 | bytes 2000000 | tf_op jit(solution)/shard_map/pallas_call | solution.py:554
  23.9 0.8 %copy.11 = f32[2,16,3584]{2,1,0:T(8,128)} copy(f32[2,16,3584]{2,1,0:T(8,128)S(1)} %shard_map.37) | data formatting | bytes 917504
  (4 shorter events, 0.2 us)
Async XLA Ops:
  1.1 0.9 %copy-start = (f32[64,896]{1,0:T(8,128)S(1)}, f32[64,896]{1,0:T(8,128)}, u32[]{:S(2)}) copy-start(f32[64,896]{1,0:T(8,128)} %param.4) | copy-start | bytes 688132
  2.1 0.9 %copy-start.1 = (f32[64,896]{1,0:T(8,128)S(1)}, f32[64,896]{1,0:T(8,128)}, u32[]{:S(2)}) copy-start(f32[64,896]{1,0:T(8,128)} %param.5) | copy-start | bytes 688132

commit v3 on v2

--- a/solution.py
+++ b/solution.py
@@ -247,15 +247,21 @@
 
 
 def kernel(
-    nd, nx, field, start, end, out,
-    own, received, summary, gathered, answer, boundary, edge_out, edge_in,
+    nd, nx, field_in, start_in, end_in, out,
+    field, start, end, own, received, summary, gathered, answer, boundary, edge_out, edge_in,
     middle, tall_end, tall_field, tall_out,
-    sum_send, sum_recv, ans_send, ans_recv, bulk_send, bulk_recv, edge_send, edge_recv,
+    sum_send, sum_recv, ans_send, ans_recv, bulk_send, bulk_recv, edge_send, edge_recv, load_sem,
 ):
-    used_rows = start.shape[1]
     width = out.shape[2] // nx
     tiles = width // LANES
     out_rows = out.shape[1]
+    used_rows = tiles * out_rows
+    loads = [
+        pltpu.make_async_copy(source_ref, dest_ref, load_sem.at[which])
+        for which, (source_ref, dest_ref) in enumerate(((end_in, end), (start_in, start), (field_in, field)))
+    ]
+    for load in loads:
+        load.start()
     slots = LANES // out_rows
     dep = lax.axis_index("depth")
     xr = lax.axis_index("xr")
@@ -282,9 +288,8 @@
         return pl.multiple_of((block * 4 + part) * LANES, LANES)
 
     def bulk_copy(peer, source_block, part):
-        source_ref = field.at[peer, part] if part < 2 else (start if part == START else end).at[peer]
         return pltpu.make_async_remote_copy(
-            src_ref=source_ref,
+            src_ref=own.at[pl.ds(at(peer, part), used_rows), :],
             dst_ref=received.at[pl.ds(at(source_block, part), used_rows), :],
             send_sem=bulk_send.at[peer, part],
             recv_sem=bulk_recv.at[source_block, part],
@@ -293,23 +298,33 @@
         )
 
     far_first = list(range(2, nx)) + [1]
+
+    def block_own(part):
+        for block in range(nx):
+            base = (block * 4 + part) * LANES
+            for tile in range(tiles):
+                place = (slice(block * out_rows, (block + 1) * out_rows), slice(tile * LANES, (tile + 1) * LANES))
+                piece = field[(part,) + place] if part < 2 else (start if part == START else end)[place]
+                own[base + tile * out_rows : base + (tile + 1) * out_rows, :] = piece
+
+    for load, parts in zip(loads, ((END,), (START,), (RE, IM))):
+        load.wait()
+        for part in parts:
+            block_own(part)
     pl.semaphore_wait(barrier, nd - 1 + nx - 1)
     for part in (END, START, RE, IM):
         for offset in far_first:
             bulk_copy(peer_at(offset), xr, part).start()
 
-    for block in range(nx):
-        for part in range(4):
-            base = (block * 4 + part) * LANES
-            if used_rows < LANES:
+    if used_rows < LANES:
+        for block in range(nx):
+            for part in range(4):
+                base = (block * 4 + part) * LANES
                 pad = jnp.full((LANES - used_rows, LANES), 0.0 if part < 2 else 0.89, jnp.float32)
                 received[base + used_rows : base + LANES, :] = pad
-                if part < 3:
-                    own[base + used_rows : base + LANES, :] = pad
-            if part < 3:
-                own[base : base + used_rows, :] = field[block, part] if part < 2 else start[block]
+                own[base + used_rows : base + LANES, :] = pad
     for part in range(4):
-        received[pl.ds(at(xr, part), used_rows), :] = field[xr, part] if part < 2 else (start if part == START else end)[xr]
+        received[pl.ds(at(xr, part), used_rows), :] = own[pl.ds(at(xr, part), used_rows), :]
 
     def wide(ref, part, row):
         return jnp.concatenate(
@@ -543,20 +558,17 @@
     slots = LANES // out_rows
     assert tiles <= nd and tiles <= slots and slots == SUBLANES and nx <= SUBLANES and nx % 2 == 0
 
-    def blocked(array):
-        lead = array.shape[:-2]
-        pieces = array.reshape(lead + (nx, out_rows, tiles, LANES))
-        pieces = jnp.moveaxis(jnp.swapaxes(pieces, -3, -2), len(lead), 0)
-        return pieces.reshape((nx,) + lead + (tiles * out_rows, LANES))
-
     f32 = jnp.float32
     dma = pltpu.SemaphoreType.DMA
     return pl.pallas_call(
         functools.partial(kernel, nd, nx),
         out_shape=jax.ShapeDtypeStruct((2, out_rows, width * nx), f32),
-        in_specs=[pl.BlockSpec(memory_space=pltpu.VMEM)] * 3,
+        in_specs=[pl.BlockSpec(memory_space=pltpu.HBM)] * 3,
         out_specs=pl.BlockSpec(memory_space=pltpu.VMEM),
         scratch_shapes=[
+            pltpu.VMEM((2, rows, width), f32),
+            pltpu.VMEM((rows, width), f32),
+            pltpu.VMEM((rows, width), f32),
             pltpu.VMEM((nx * 4 * LANES, LANES), f32),
             pltpu.VMEM((nx * 4 * LANES, LANES), f32),
             pltpu.VMEM((slots * SUMMARY_ROWS, LANES), f32),
@@ -577,12 +589,13 @@
             dma((nx, 4)),
             dma((nx,)),
             dma((nx,)),
+            dma((3,)),
         ],
         compiler_params=pltpu.CompilerParams(
-            collective_id=0, has_side_effects=True, vmem_limit_bytes=32 * 1024 * 1024
+            collective_id=0, has_side_effects=True, vmem_limit_bytes=64 * 1024 * 1024
         ),
         cost_estimate=pl.CostEstimate(flops=20_000_000, bytes_accessed=2_000_000, transcendentals=0),
-    )(blocked(sound_field), blocked(index_start), blocked(index_end))
+    )(sound_field, index_start, index_end)
 
 
 def solution(mesh):

time: 24.9 us -> 23.6 us (0.948)
  local copies, waits for them, and re-layouts: 3.82 us -> 1.82 us
  Pallas kernels: 20.8 us -> 21.6 us
    reshape x3 -> x0, local copies, waits for them, and re-layouts: 1.16 us -> none  [blocked(): pieces = array.reshape(lead + (nx, out_rows, tiles, LANES))]
    pallas_call x1, Pallas kernels: 20.8 us -> 21.6 us  [local(): pl.pallas_call(functools.partial(kernel, nd, nx), out_shape=jax.ShapeDtyp...]
    unnamed x5 -> x1, local copies, waits for them, and re-layouts: 2.49 us -> 1.82 us
where the time goes in v3:
time: 23.6 us; the launch traced here: 23.4 us
  Pallas kernels  21.6 us (92%)
  local copies, waits for them, and re-layouts  1.82 us (8%)
    pallas_call x1, Pallas kernels, local(): pl.pallas_call(functools.partial(kernel, nd, nx), out_shape=jax.ShapeDtyp...  21.6 us
    unnamed x1, local copies, waits for them, and re-layouts  1.82 us

profile of v3, /device:TPU:0, one launch (start us, length us, event | category | flops | bytes accessed | tf_op | source)
XLA Modules:
  0.0 23.4 jit_solution(17786863648693226725)
XLA Ops:
  0.0 21.6 %shard_map.37 = f32[2,16,3584]{2,1,0:T(8,128)} custom-call(f32[2,64,896]{2,1,0:T(8,128)} %field_in.1, f32[64,896]{1,0:T(8,128)} %start_in.1, f32[64,896]{1,0:T(8,128)} %end_in.1), custom_call_target="tpu_custom_call" | custom-call | flops 20000000 | bytes 2000000 | tf_op jit(solution)/shard_map/pallas_call | solution.py:563
  21.6 1.8 %copy.5 = f32[2,16,3584]{2,1,0:T(8,128)} copy(f32[2,16,3584]{2,1,0:T(8,128)} %shard_map.37) | data formatting | bytes 917504

commit v4 on v3

--- a/solution.py
+++ b/solution.py
@@ -247,21 +247,15 @@
 
 
 def kernel(
-    nd, nx, field_in, start_in, end_in, out,
-    field, start, end, own, received, summary, gathered, answer, boundary, edge_out, edge_in,
+    nd, nx, field, start, end, out,
+    own, received, summary, gathered, answer, boundary, edge_out, edge_in,
     middle, tall_end, tall_field, tall_out,
-    sum_send, sum_recv, ans_send, ans_recv, bulk_send, bulk_recv, edge_send, edge_recv, load_sem,
+    sum_send, sum_recv, ans_send, ans_recv, bulk_send, bulk_recv, edge_send, edge_recv,
 ):
     width = out.shape[2] // nx
     tiles = width // LANES
     out_rows = out.shape[1]
     used_rows = tiles * out_rows
-    loads = [
-        pltpu.make_async_copy(source_ref, dest_ref, load_sem.at[which])
-        for which, (source_ref, dest_ref) in enumerate(((end_in, end), (start_in, start), (field_in, field)))
-    ]
-    for load in loads:
-        load.start()
     slots = LANES // out_rows
     dep = lax.axis_index("depth")
     xr = lax.axis_index("xr")
@@ -307,10 +301,8 @@
                 piece = field[(part,) + place] if part < 2 else (start if part == START else end)[place]
                 own[base + tile * out_rows : base + (tile + 1) * out_rows, :] = piece
 
-    for load, parts in zip(loads, ((END,), (START,), (RE, IM))):
-        load.wait()
-        for part in parts:
-            block_own(part)
+    for part in (END, START, RE, IM):
+        block_own(part)
     pl.semaphore_wait(barrier, nd - 1 + nx - 1)
     for part in (END, START, RE, IM):
         for offset in far_first:
@@ -563,12 +555,9 @@
     return pl.pallas_call(
         functools.partial(kernel, nd, nx),
         out_shape=jax.ShapeDtypeStruct((2, out_rows, width * nx), f32),
-        in_specs=[pl.BlockSpec(memory_space=pltpu.HBM)] * 3,
+        in_specs=[pl.BlockSpec(memory_space=pltpu.VMEM)] * 3,
         out_specs=pl.BlockSpec(memory_space=pltpu.VMEM),
         scratch_shapes=[
-            pltpu.VMEM((2, rows, width), f32),
-            pltpu.VMEM((rows, width), f32),
-            pltpu.VMEM((rows, width), f32),
             pltpu.VMEM((nx * 4 * LANES, LANES), f32),
             pltpu.VMEM((nx * 4 * LANES, LANES), f32),
             pltpu.VMEM((slots * SUMMARY_ROWS, LANES), f32),
@@ -589,10 +578,9 @@
             dma((nx, 4)),
             dma((nx,)),
             dma((nx,)),
-            dma((3,)),
         ],
         compiler_params=pltpu.CompilerParams(
-            collective_id=0, has_side_effects=True, vmem_limit_bytes=64 * 1024 * 1024
+            collective_id=0, has_side_effects=True, vmem_limit_bytes=32 * 1024 * 1024
         ),
         cost_estimate=pl.CostEstimate(flops=20_000_000, bytes_accessed=2_000_000, transcendentals=0),
     )(sound_field, index_start, index_end)

time: 23.6 us -> 24.7 us (1.047)
  local copies, waits for them, and re-layouts: 1.82 us -> 3.66 us
  Pallas kernels: 21.6 us -> 20.8 us
    unnamed x1 -> x7, local copies, waits for them, and re-layouts: 1.82 us -> 3.66 us
    pallas_call x1, Pallas kernels: 21.6 us -> 20.8 us  [local(): pl.pallas_call(functools.partial(kernel, nd, nx), out_shape=jax.ShapeDtyp...]
where the time goes in v4:
time: 24.7 us; the launch traced here: 24.5 us
  Pallas kernels  20.8 us (84%)
  local copies, waits for them, and re-layouts  3.66 us (15%)
    pallas_call x1, Pallas kernels, local(): pl.pallas_call(functools.partial(kernel, nd, nx), out_shape=jax.ShapeDtyp...  20.8 us
    unnamed x7, local copies, waits for them, and re-layouts  3.66 us

profile of v4, /device:TPU:0, one launch (start us, length us, event | category | flops | bytes accessed | tf_op | source)
XLA Modules:
  0.0 24.5 jit_solution(5195749180621773107)
XLA Ops:
  0.0 0.0 copy-start
  0.0 1.0 %copy-done = f32[2,64,896]{2,1,0:T(8,128)S(1)} copy-done((f32[2,64,896]{2,1,0:T(8,128)S(1)}, f32[2,64,896]{2,1,0:T(8,128)}, u32[]{:S(2)}) %copy-start) | copy-done | bytes 458776
  1.0 0.0 copy-start.1
  1.0 0.9 %copy-done.1 = f32[64,896]{1,0:T(8,128)S(1)} copy-done((f32[64,896]{1,0:T(8,128)S(1)}, f32[64,896]{1,0:T(8,128)}, u32[]{:S(2)}) %copy-start.1) | copy-done | bytes 229400
  2.0 0.0 copy-start.2
  2.0 0.9 %copy-done.2 = f32[64,896]{1,0:T(8,128)S(1)} copy-done((f32[64,896]{1,0:T(8,128)S(1)}, f32[64,896]{1,0:T(8,128)}, u32[]{:S(2)}) %copy-start.2) | copy-done | bytes 229400
  2.9 20.8 %shard_map.37 = f32[2,16,3584]{2,1,0:T(8,128)S(1)} custom-call(f32[2,64,896]{2,1,0:T(8,128)S(1)} %copy-done, f32[64,896]{1,0:T(8,128)S(1)} %copy-done.1, f32[64,896]{1,0:T(8,128)S(1)} %copy-done.2), custom_call_target="tpu_custom_call" | custom-call | flops 20000000 | bytes 2000000 | tf_op jit(solution)/shard_map/pallas_call | solution.py:555
  23.7 0.8 %copy.5 = f32[2,16,3584]{2,1,0:T(8,128)} copy(f32[2,16,3584]{2,1,0:T(8,128)S(1)} %shard_map.37) | data formatting | bytes 917504
Async XLA Ops:
  0.0 1.0 %copy-start = (f32[2,64,896]{2,1,0:T(8,128)S(1)}, f32[2,64,896]{2,1,0:T(8,128)}, u32[]{:S(2)}) copy-start(f32[2,64,896]{2,1,0:T(8,128)} %field.1) | copy-start | bytes 1376260
  1.0 0.9 %copy-start.1 = (f32[64,896]{1,0:T(8,128)S(1)}, f32[64,896]{1,0:T(8,128)}, u32[]{:S(2)}) copy-start(f32[64,896]{1,0:T(8,128)} %start.1) | copy-start | bytes 688132
  2.0 0.9 %copy-start.2 = (f32[64,896]{1,0:T(8,128)S(1)}, f32[64,896]{1,0:T(8,128)}, u32[]{:S(2)}) copy-start(f32[64,896]{1,0:T(8,128)} %end.1) | copy-start | bytes 688132

commit v5 on v4

--- a/solution.py
+++ b/solution.py
@@ -297,8 +297,8 @@
         for block in range(nx):
             base = (block * 4 + part) * LANES
             for tile in range(tiles):
-                place = (slice(block * out_rows, (block + 1) * out_rows), slice(tile * LANES, (tile + 1) * LANES))
-                piece = field[(part,) + place] if part < 2 else (start if part == START else end)[place]
+                place = slice(block * out_rows, (block + 1) * out_rows)
+                piece = field[tile, part, place] if part < 2 else (start if part == START else end)[tile, place]
                 own[base + tile * out_rows : base + (tile + 1) * out_rows, :] = piece
 
     for part in (END, START, RE, IM):
@@ -550,6 +550,9 @@
     slots = LANES // out_rows
     assert tiles <= nd and tiles <= slots and slots == SUBLANES and nx <= SUBLANES and nx % 2 == 0
 
+    field = sound_field.reshape(2, rows, tiles, LANES).transpose(2, 0, 1, 3)
+    start = index_start.reshape(rows, tiles, LANES).transpose(1, 0, 2)
+    end = index_end.reshape(rows, tiles, LANES).transpose(1, 0, 2)
     f32 = jnp.float32
     dma = pltpu.SemaphoreType.DMA
     return pl.pallas_call(
@@ -583,7 +586,7 @@
             collective_id=0, has_side_effects=True, vmem_limit_bytes=32 * 1024 * 1024
         ),
         cost_estimate=pl.CostEstimate(flops=20_000_000, bytes_accessed=2_000_000, transcendentals=0),
-    )(sound_field, index_start, index_end)
+    )(field, start, end)
 
 
 def solution(mesh):

time: 24.7 us -> 23 us (0.931)
  local copies, waits for them, and re-layouts: 3.66 us -> 1.98 us
    unnamed x7, local copies, waits for them, and re-layouts: 3.66 us -> 1.91 us
where the time goes in v5:
time: 23 us; the launch traced here: 22.8 us
  Pallas kernels  20.8 us (90%)
  local copies, waits for them, and re-layouts  1.98 us (9%)
    pallas_call x1, Pallas kernels, local(): pl.pallas_call(functools.partial(kernel, nd, nx), out_shape=jax.ShapeDtyp...  20.8 us
    unnamed x7, local copies, waits for them, and re-layouts  1.91 us

profile of v5, /device:TPU:0, one launch (start us, length us, event | category | flops | bytes accessed | tf_op | source)
XLA Modules:
  0.0 22.8 jit_solution(17381117680493418518)
XLA Ops:
  0.0 0.0 copy-start
  0.0 0.0 copy-start.2
  0.0 0.0 copy-start.1
  0.0 1.0 %copy-done = f32[2,64,896]{2,1,0:T(8,128)S(1)} copy-done((f32[2,64,896]{2,1,0:T(8,128)S(1)}, f32[2,64,896]{2,1,0:T(8,128)}, u32[]{:S(2)}) %copy-start) | copy-done | bytes 458776
  1.1 0.0 copy-done.2
  1.1 0.1 copy-done.1
  1.2 20.8 %shard_map.37 = f32[2,16,3584]{2,1,0:T(8,128)S(1)} custom-call(f32[7,2,64,128]{3,2,1,0:T(8,128)S(1)} %bitcast_bitcast_fusion.field, f32[7,64,128]{2,1,0:T(8,128)S(1)} %get-tuple-element.6.start, f32[7,64,128]{2,1,0:T(8,128)S(1)} %get-tuple-element.5.end), custom_call_target="tpu_custom_call" | custom-call | flops 20000000 | bytes 2000000 | tf_op jit(solution)/shard_map/pallas_call | solution.py:558
  22.1 0.8 %copy.14 = f32[2,16,3584]{2,1,0:T(8,128)} copy(f32[2,16,3584]{2,1,0:T(8,128)S(1)} %shard_map.37) | data formatting | bytes 917504
  (2 shorter events, 0.1 us)
Async XLA Ops:
  0.0 1.0 %copy-start = (f32[2,64,896]{2,1,0:T(8,128)S(1)}, f32[2,64,896]{2,1,0:T(8,128)}, u32[]{:S(2)}) copy-start(f32[2,64,896]{2,1,0:T(8,128)} %param.3) | copy-start | bytes 1376260
  0.0 1.1 %copy-start.2 = (f32[64,896]{1,0:T(8,128)S(1)}, f32[64,896]{1,0:T(8,128)}, u32[]{:S(2)}) copy-start(f32[64,896]{1,0:T(8,128)} %param.5) | copy-start | bytes 688132
  0.0 1.2 %copy-start.1 = (f32[64,896]{1,0:T(8,128)S(1)}, f32[64,896]{1,0:T(8,128)}, u32[]{:S(2)}) copy-start(f32[64,896]{1,0:T(8,128)} %param.4) | copy-start | bytes 688132
